TPU v7x, 256 devices: a whole 4x4x8 slice. The times are simulated.
256 devices in a mesh: member: 8 (over y, z_hi), grid: 32 (over x, z_lo, core).
Axes of the slice: x: 4, y: 4, z: 8 (z_hi: 2, z_lo: 4; z = z_hi * 4 + z_lo), core: 2. Of those that a mesh axis runs over, the one named last changes fastest.
Arguments:
- hidden: bfloat16 [8, 65536, 1024], P('member', 'grid'), may hold values from -6 to 6
- pred: bfloat16 [8, 100, 65536], P('member', None, 'grid'), may hold values from -6 to 6
- target: bfloat16 [100, 65536], P(None, 'grid'), may hold values from -6 to 6
- area: float32 [65536], P('grid'), may hold values from 0.5 to 5
- var_weight: float32 [100], replicated, may hold values from 0.5 to 5
- w_in: bfloat16 [1024, 1024], replicated, may hold values from -0.1875 to 0.1875
- w_out: bfloat16 [1024, 100], replicated, may hold values from -0.1875 to 0.1875
Outputs:
- hidden_grad: bfloat16 [8, 65536, 1024], P('member', 'grid')
- w_in_grad: float32 [1024, 1024], P('grid')
- w_out_grad: float32 [1024, 100], P('grid')
All inputs are finite; a program needn't handle non-finite values.
Results may differ from a plain program's by a relative error of at most 0.0061.
Values may be sent and summed in bfloat16 or wider, within the bound.
A program may use at most 128 MiB of HBM per device.

v0:
```python
import math

import jax
import jax.numpy as jnp
from jax import lax
from jax.sharding import PartitionSpec as P


def shifted(value, axis, steps):
    count = lax.axis_size(axis)
    pairs = [(source, (source + steps) % count) for source in range(count)]
    return lax.ppermute(value, axis, pairs)


def shards(hidden, pred, target, area, var_weight, w_in, w_out):
    members = lax.axis_size("member")
    grid_count = lax.axis_size("grid")
    own_pred = pred[0]
    preds = own_pred.astype(jnp.float32)
    weight = var_weight[:, None] * area[None, :]
    spread = jnp.zeros(preds.shape, jnp.float32)
    for offset in range(1, members // 2 + 1):
        partner = shifted(own_pred, "member", offset)
        term = (weight * jnp.sign(preds - partner.astype(jnp.float32))).astype(jnp.bfloat16)
        spread = spread + lax.optimization_barrier(term).astype(jnp.float32)
        if 2 * offset < members:
            back = shifted(term, "member", -offset)
            spread = spread - back.astype(jnp.float32)
    grad = weight * jnp.sign(preds - target.astype(jnp.float32)) / members
    grad = (grad - spread / (members * (members - 1))).astype(jnp.bfloat16)
    rows = hidden[0]
    pre = jnp.dot(rows, w_in, preferred_element_type=jnp.float32)
    act = jax.nn.gelu(pre).astype(jnp.bfloat16)
    act_grad = lax.dot_general(
        grad, w_out, (((0,), (1,)), ((), ())), preferred_element_type=jnp.float32
    )
    pre_grad = jax.vjp(jax.nn.gelu, pre)[1](act_grad)[0].astype(jnp.bfloat16)
    rows_grad = lax.dot_general(
        pre_grad, w_in, (((1,), (1,)), ((), ())), preferred_element_type=jnp.float32
    )
    hidden_grad = rows_grad.astype(jnp.bfloat16)[None]
    scale = 1.0 / math.sqrt(rows.shape[0] * grid_count * members)
    width = w_in.shape[0]
    share = width // grid_count
    in_term = lax.dot_general(
        rows, pre_grad, (((0,), (0,)), ((), ())), preferred_element_type=jnp.float32
    )
    out_term = lax.dot_general(
        act, grad, (((0,), (1,)), ((), ())), preferred_element_type=jnp.float32
    )
    in_sum, out_sum = lax.psum((in_term, out_term), ("member", "grid"))
    first = lax.axis_index("grid") * share
    in_rows = lax.dynamic_slice_in_dim(in_sum, first, share, 0)
    out_rows = lax.dynamic_slice_in_dim(out_sum, first, share, 0)
    return (hidden_grad, in_rows * scale, out_rows * scale)


def solution(mesh):
    return jax.shard_map(
        shards,
        mesh=mesh,
        in_specs=(
            P("member", "grid", None),
            P("member", None, "grid"),
            P(None, "grid"),
            P("grid"),
            P(),
            P(),
            P(),
        ),
        out_specs=(P("member", "grid", None), P("grid", None), P("grid", None)),
        check_vma=False,
    )
```

profile of v0, /device:TPU:32, one launch (start us, length us, event | category | flops | bytes accessed | tf_op | source)
XLA Modules:
  0.0 397.6 jit_solution(8837434357494850661)
XLA Ops:
  7.2 0.0 copy-start
  7.2 0.0 all-reduce.3.cloned.1.call-start
  7.2 6.4 %collective-permute-start = (bf16[100,2048]{1,0:T(8,128)(2,1)}, bf16[100,2048]{1,0:T(8,128)(2,1)S(1)}, u32[]{:S(2)}, u32[]{:S(2)}) collective-permute-start(bf16[100,2048]{1,0:T(8,128)(2,1)} %bitcast.24), channel_id=1, source_target_pairs={{0,32},{32,64},{64,96},{96,128},{128,160},{160,192},{192,224},{224... | collective-permute-start | bytes 1228808 | tf_op jit(solution)/shard_map/ppermute | solution.py:12
  13.6 1.6 collective-permute-start.2
  15.2 1.4 collective-permute-start.4
  16.5 1.8 collective-permute-start.6
  18.4 26.0 %collective-permute-done = bf16[100,2048]{1,0:T(8,128)(2,1)S(1)} collective-permute-done((bf16[100,2048]{1,0:T(8,128)(2,1)}, bf16[100,2048]{1,0:T(8,128)(2,1)S(1)}, u32[]{:S(2)}, u32[]{:S(2)}) %collective-permute-start) | collective-permute-done | bytes 409632 | tf_op jit(solution)/shard_map/ppermute | solution.py:12
  44.4 0.0 collective-permute-done.2
  44.4 5.9 %collective-permute-done.4 = bf16[100,2048]{1,0:T(8,128)(2,1)S(1)} collective-permute-done((bf16[100,2048]{1,0:T(8,128)(2,1)}, bf16[100,2048]{1,0:T(8,128)(2,1)S(1)}, u32[]{:S(2)}, u32[]{:S(2)}) %collective-permute-start.4) | collective-permute-done | bytes 409632 | tf_op jit(solution)/shard_map/ppermute | solution.py:12
  50.3 5.4 %collective-permute-done.6 = bf16[100,2048]{1,0:T(8,128)(2,1)S(1)} collective-permute-done((bf16[100,2048]{1,0:T(8,128)(2,1)}, bf16[100,2048]{1,0:T(8,128)(2,1)S(1)}, u32[]{:S(2)}, u32[]{:S(2)}) %collective-permute-start.6) | collective-permute-done | bytes 409632 | tf_op jit(solution)/shard_map/ppermute | solution.py:12
  55.7 2.3 fusion.23
  58.0 0.1 collective-permute-start.1
  58.0 0.1 collective-permute-start.3
  58.1 0.0 copy-start.1
  58.2 0.0 copy-start.2
  58.2 0.0 copy-start.3
  58.2 0.0 copy-start.4
  58.2 6.6 %collective-permute-start.5 = (bf16[100,2048]{1,0:T(8,128)(2,1)S(1)}, bf16[100,2048]{1,0:T(8,128)(2,1)S(1)}, u32[]{:S(2)}, u32[]{:S(2)}) collective-permute-start(bf16[100,2048]{1,0:T(8,128)(2,1)S(1)} %get-tuple-element.10), channel_id=1, source_target_pairs={{0,160},{32,192},{64,224},{96,0},{128,32},{160,64},{192,96},{224,1... | collective-permute-start | bytes 1228808 | tf_op jit(solution)/shard_map/ppermute | solution.py:12
  64.8 0.0 copy-done
  64.8 6.3 %fusion.9 = f32[2048,1024]{1,0:T(8,128)S(1)} fusion(bf16[1024,1024]{1,0:T(8,128)(2,1)S(1)} %copy-done, bf16[1,2048,1024]{2,1,0:T(8,128)(2,1)} %param.7), kind=kOutput, calls=%fused_computation.12 | convolution fusion | flops 4294967296 | bytes 14680064 | tf_op jit(solution)/shard_map/dot_general | solution.py:32
  71.1 6.4 %collective-permute-done.1 = bf16[100,2048]{1,0:T(8,128)(2,1)S(1)} collective-permute-done((bf16[100,2048]{1,0:T(8,128)(2,1)S(1)}, bf16[100,2048]{1,0:T(8,128)(2,1)S(1)}, u32[]{:S(2)}, u32[]{:S(2)}) %collective-permute-start.1) | collective-permute-done | bytes 409632 | tf_op jit(solution)/shard_map/ppermute | solution.py:12
  77.5 0.0 collective-permute-done.3
  77.5 20.1 %collective-permute-done.5 = bf16[100,2048]{1,0:T(8,128)(2,1)S(1)} collective-permute-done((bf16[100,2048]{1,0:T(8,128)(2,1)S(1)}, bf16[100,2048]{1,0:T(8,128)(2,1)S(1)}, u32[]{:S(2)}, u32[]{:S(2)}) %collective-permute-start.5) | collective-permute-done | bytes 409632 | tf_op jit(solution)/shard_map/ppermute | solution.py:12
  97.6 0.0 copy-done.1
  97.6 0.0 copy-done.2
  97.6 0.0 copy-done.3
  97.6 0.0 copy-done.4
  97.6 0.8 fusion.22
  98.4 0.0 copy-start.6
  98.4 3.8 fusion.11
  102.2 0.0 copy-done.6
  102.2 0.0 copy-start.5
  102.2 6.3 %fusion.6 = bf16[2048,1024]{1,0:T(8,128)(2,1)S(1)} fusion(f32[2048,1024]{1,0:T(8,128)S(1)} %fusion.9, bf16[100,2048]{1,0:T(8,128)(2,1)S(1)} %fusion.22, bf16[1024,100]{0,1:T(8,128)(2,1)S(1)} %copy-done.6), kind=kOutput, calls=%fused_computation.8 | convolution fusion | flops 461373440 | bytes 13197312 | tf_op jit(solution)/shard_map/dot_general | solution.py:34
  108.6 0.0 copy-start.7
  108.6 2.0 copy-done.7
  110.5 0.0 copy-done.5
  110.5 6.2 %fusion.12 = f32[1024,1024]{0,1:T(8,128)} fusion(bf16[2048,1024]{1,0:T(8,128)(2,1)S(1)} %fusion.6, bf16[1,2048,1024]{2,1,0:T(8,128)(2,1)S(1)} %copy-done.5), kind=kOutput, calls=%fused_computation.21 | convolution fusion | flops 4294967296 | bytes 12582912 | tf_op jit(solution)/shard_map/dot_general | solution.py:45
  116.7 0.0 all-reduce.3.cloned.1.call-update
  116.7 8.3 %convert_bitcast_fusion = bf16[1,2048,1024]{2,1,0:T(8,128)(2,1)} fusion(bf16[2048,1024]{1,0:T(8,128)(2,1)} %copy-done.7, bf16[1024,1024]{1,0:T(8,128)(2,1)S(1)} %copy-done), kind=kOutput, calls=%fused_computation.14 | convolution fusion | flops 4297064448 | bytes 10485760 | tf_op jit(solution)/shard_map/dot_general | solution.py:38
  125.0 262.3 %all-reduce.3.cloned.1.call-done = (f32[1024,1024]{0,1:T(8,128)}, f32[1024,100]{1,0:T(8,128)}) async-done(((f32[1024,1024]{0,1:T(8,128)}, f32[1024,100]{1,0:T(8,128)}), (f32[1024,1024]{0,1:T(8,128)}, f32[1024,100]{1,0:T(8,128)})) %all-reduce.3.cloned.1.call-update) | async-done | bytes 4603920 | tf_op jit(solution)/shard_map/psum | solution.py:51
  387.3 1.2 dynamic-slice_multiply_fusion
  388.6 0.8 copy.10
  389.4 1.3 dynamic-slice_multiply_fusion.1
Async XLA Ops:
  7.2 57.7 %copy-start = (bf16[1024,1024]{1,0:T(8,128)(2,1)S(1)}, bf16[1024,1024]{1,0:T(8,128)(2,1)}, u32[]{:S(2)}) copy-start(bf16[1024,1024]{1,0:T(8,128)(2,1)} %param.12) | copy-start | bytes 6291460
  7.2 380.2 %all-reduce.3.cloned.1.call-start = ((), (), s32[]{:S(2)}) async-start(), calls=%async_computation | async-start | bytes 9437184 | tf_op jit(solution)/shard_map/psum | solution.py:51
  7.2 37.1 %collective-permute-start = (bf16[100,2048]{1,0:T(8,128)(2,1)}, bf16[100,2048]{1,0:T(8,128)(2,1)S(1)}, u32[]{:S(2)}, u32[]{:S(2)}) collective-permute-start(bf16[100,2048]{1,0:T(8,128)(2,1)} %bitcast.24), channel_id=1, source_target_pairs={{0,32},{32,64},{64,96},{96,128},{128,160},{160,192},{192,224},{224... | collective-permute-start | bytes 1228808 | tf_op jit(solution)/shard_map/ppermute | solution.py:12
  13.6 30.8 %collective-permute-start.2 = (bf16[100,2048]{1,0:T(8,128)(2,1)}, bf16[100,2048]{1,0:T(8,128)(2,1)S(1)}, u32[]{:S(2)}, u32[]{:S(2)}) collective-permute-start(bf16[100,2048]{1,0:T(8,128)(2,1)} %bitcast.25), channel_id=1, source_target_pairs={{0,64},{32,96},{64,128},{96,160},{128,192},{160,224},{192,0},{224,... | collective-permute-start | bytes 1228808 | tf_op jit(solution)/shard_map/ppermute | solution.py:12
  15.2 35.1 %collective-permute-start.4 = (bf16[100,2048]{1,0:T(8,128)(2,1)}, bf16[100,2048]{1,0:T(8,128)(2,1)S(1)}, u32[]{:S(2)}, u32[]{:S(2)}) collective-permute-start(bf16[100,2048]{1,0:T(8,128)(2,1)} %bitcast.26), channel_id=1, source_target_pairs={{0,96},{32,128},{64,160},{96,192},{128,224},{160,0},{192,32},{224,... | collective-permute-start | bytes 1228808 | tf_op jit(solution)/shard_map/ppermute | solution.py:12
  16.5 39.1 %collective-permute-start.6 = (bf16[100,2048]{1,0:T(8,128)(2,1)}, bf16[100,2048]{1,0:T(8,128)(2,1)S(1)}, u32[]{:S(2)}, u32[]{:S(2)}) collective-permute-start(bf16[100,2048]{1,0:T(8,128)(2,1)} %bitcast.27), channel_id=1, source_target_pairs={{0,128},{32,160},{64,192},{96,224},{128,0},{160,32},{192,64},{224,... | collective-permute-start | bytes 1228808 | tf_op jit(solution)/shard_map/ppermute | solution.py:12
  58.0 19.5 %collective-permute-start.1 = (bf16[100,2048]{1,0:T(8,128)(2,1)S(1)}, bf16[100,2048]{1,0:T(8,128)(2,1)S(1)}, u32[]{:S(2)}, u32[]{:S(2)}) collective-permute-start(bf16[100,2048]{1,0:T(8,128)(2,1)S(1)} %get-tuple-element.8), channel_id=1, source_target_pairs={{0,224},{32,0},{64,32},{96,64},{128,96},{160,128},{192,160},{224,1... | collective-permute-start | bytes 1228808 | tf_op jit(solution)/shard_map/ppermute | solution.py:12
  58.0 19.4 %collective-permute-start.3 = (bf16[100,2048]{1,0:T(8,128)(2,1)S(1)}, bf16[100,2048]{1,0:T(8,128)(2,1)S(1)}, u32[]{:S(2)}, u32[]{:S(2)}) collective-permute-start(bf16[100,2048]{1,0:T(8,128)(2,1)S(1)} %get-tuple-element.11), channel_id=1, source_target_pairs={{0,192},{32,224},{64,0},{96,32},{128,64},{160,96},{192,128},{224,1... | collective-permute-start | bytes 1228808 | tf_op jit(solution)/shard_map/ppermute | solution.py:12
  58.1 39.4 %copy-start.1 = (bf16[1,100,2048]{2,1,0:T(8,128)(2,1)S(1)}, bf16[1,100,2048]{2,1,0:T(8,128)(2,1)}, u32[]{:S(2)}) copy-start(bf16[1,100,2048]{2,1,0:T(8,128)(2,1)} %param.8) | copy-start | bytes 1228804
  58.2 39.4 %copy-start.2 = (bf16[100,2048]{1,0:T(8,128)(2,1)S(1)}, bf16[100,2048]{1,0:T(8,128)(2,1)}, u32[]{:S(2)}) copy-start(bf16[100,2048]{1,0:T(8,128)(2,1)} %param.9) | copy-start | bytes 1228804
  58.2 39.4 %copy-start.3 = (f32[2048]{0:T(1024)S(1)}, f32[2048]{0:T(1024)}, u32[]{:S(2)}) copy-start(f32[2048]{0:T(1024)} %param.10) | copy-start | bytes 24580
  58.2 39.4 %copy-start.4 = (f32[100]{0:T(128)S(1)}, f32[100]{0:T(128)}, u32[]{:S(2)}) copy-start(f32[100]{0:T(128)} %param.11) | copy-start | bytes 1204
  58.2 39.4 %collective-permute-start.5 = (bf16[100,2048]{1,0:T(8,128)(2,1)S(1)}, bf16[100,2048]{1,0:T(8,128)(2,1)S(1)}, u32[]{:S(2)}, u32[]{:S(2)}) collective-permute-start(bf16[100,2048]{1,0:T(8,128)(2,1)S(1)} %get-tuple-element.10), channel_id=1, source_target_pairs={{0,160},{32,192},{64,224},{96,0},{128,32},{160,64},{192,96},{224,1... | collective-permute-start | bytes 1228808 | tf_op jit(solution)/shard_map/ppermute | solution.py:12
  98.4 3.8 copy-start.6
  102.2 8.3 %copy-start.5 = (bf16[1,2048,1024]{2,1,0:T(8,128)(2,1)S(1)}, bf16[1,2048,1024]{2,1,0:T(8,128)(2,1)}, u32[]{:S(2)}) copy-start(bf16[1,2048,1024]{2,1,0:T(8,128)(2,1)} %param.7) | copy-start | bytes 12582916
  108.6 2.0 copy-start.7
Sparse Core Ops, SparseCore 0:
  116.8 270.4 all-reduce.2
where the time goes:
time: 401 us; the launch traced here: 398 us
  waiting for transfers between devices  326 us (81%)
  matrix products  30.9 us (8%)
  starting transfers between devices  18 us (4%)
  between operations  14.2 us (4%)
  other arithmetic  5.64 us (1%)
    psum x1, waiting for transfers between devices, shards(): in_sum, out_sum = lax.psum((in_term, out_term), ('member', 'grid'))  262 us
    ppermute x7, waiting for transfers between devices, shifted(): return lax.ppermute(value, axis, pairs)  63.8 us
    ppermute x7, starting transfers between devices, shifted(): return lax.ppermute(value, axis, pairs)  18 us
    dot_general x1, matrix products, shards(): lax.dot_general(pre_grad, w_in, (((1,), (1,)), ((), ())), preferred_eleme...  8.31 us
  transfers between devices with their start and end apart: 8, of which 6 were waited for; matrix products, arithmetic and copies ran while one was open for 4% of the time, Pallas kernels for 0%

commit v1 on v0

v1 whole, which is shorter than its diff:
```python
import functools
import math

import jax
import jax.numpy as jnp
from jax import lax
from jax.experimental import pallas as pl
from jax.experimental.pallas import tpu as pltpu
from jax.sharding import PartitionSpec as P

BF = jnp.bfloat16
F32 = jnp.float32
MEMBERS = 8
V = 100
VS = 112
VP = 128
NCH = 2
BLK = 256
WB = 512
NWB = 2
ROOT = math.sqrt(2.0 / math.pi)


def dot(a, b):
    return jnp.dot(a, b, preferred_element_type=F32)


def dot_nt(a, b):
    return lax.dot_general(a, b, (((1,), (1,)), ((), ())), preferred_element_type=F32)


def kernel(
    scale,
    hid_hbm, pred_hbm, tgt_hbm, area, vw, win_hbm, wout,
    hg_hbm, win_out, wout_out,
    hid, win, hT, act, gp, pg, hgs, wop, woT,
    prcv, tgt, gout, gbuf,
    csnd, crcv, own, cosnd, corcv, oown,
    s1, s1o, r1a, r1b, r1o, a2, b2,
    s2a, s2b, r2a, r2b, s3, r3, s4, r4,
    lsem, hsem, osem, psem, gsem, csem, x1sem, y1sem, o1sem, a2sem, b2sem, z3sem, y4sem,
):
    points = hid.shape[0]
    width = hid.shape[1]
    half = points // NCH
    m = lax.axis_index("member")
    g = lax.axis_index("grid")
    y, z_hi = m // 2, m % 2
    x, z_lo, core = g // 8, (g // 2) % 4, g % 2
    z = z_hi * 4 + z_lo

    def dev(xx, yy, zz, cc):
        return (yy * 2 + zz // 4, (xx * 4 + zz % 4) * 2 + cc)

    def member_dev(mm):
        return (mm, g)

    def remote(src, dst, sems, j, target):
        return pltpu.make_async_remote_copy(
            src_ref=src, dst_ref=dst, send_sem=sems.at[0, j], recv_sem=sems.at[1, j],
            device_id=target, device_id_type=pl.DeviceIdType.MESH,
        )

    barrier = pltpu.get_barrier_semaphore()
    partners = [member_dev((m + j) % MEMBERS) for j in range(1, MEMBERS)]
    partners += [dev(x, y, (z + j) % 8, core) for j in (1, 2, 3, 5, 6, 7)]
    partners += [dev((x + j) % 4, y, z, core) for j in (1, 2, 3)]
    partners += [dev(x, y, z, 1 - core)]
    for partner in partners:
        pl.semaphore_signal(barrier, inc=1, device_id=partner, device_id_type=pl.DeviceIdType.MESH)

    win_copy = pltpu.make_async_copy(win_hbm, win, lsem.at[0])
    win_copy.start()

    def hid_copy(i):
        rows = pl.ds(pl.multiple_of(i * BLK, BLK), BLK)
        return pltpu.make_async_copy(hid_hbm.at[0, rows], hid.at[rows], hsem.at[i])

    hid_copy(0).start()
    own_copies = []
    for c in range(NCH):
        cols = pl.ds(pl.multiple_of(c * half + 128 * m, 128), 128)
        own_copies.append(pltpu.make_async_copy(pred_hbm.at[0, :, cols], prcv.at[c, m], lsem.at[1 + 2 * c]))
        own_copies.append(pltpu.make_async_copy(tgt_hbm.at[:, cols], tgt.at[c], lsem.at[2 + 2 * c]))
    for copy in own_copies:
        copy.start()
    for i in range(1, points // BLK):
        hid_copy(i).start()

    gbuf[...] = jnp.zeros_like(gbuf)
    gout[...] = jnp.zeros_like(gout)
    wop[...] = jnp.zeros_like(wop)
    wop[:, :V] = wout[...]
    woT[...] = jnp.transpose(wop[...])
    rows_at = lax.broadcasted_iota(jnp.int32, (V, V), 0)
    cols_at = lax.broadcasted_iota(jnp.int32, (V, V), 1)
    vcol = jnp.sum(jnp.where(rows_at == cols_at, jnp.broadcast_to(vw[...], (V, V)), 0.0), axis=1, keepdims=True)
    win_copy.wait()

    def forward(i, carry):
        hid_copy(i).wait()
        rows = pl.ds(pl.multiple_of(i * BLK, BLK), BLK)
        h = hid[rows, :]
        for n in range(0, width, 256):
            u = dot(h, win[:, n:n + 256])
            square = u * u
            t = jnp.tanh(u * (square * (ROOT * 0.044715) + ROOT))
            p = 0.5 * t + 0.5
            a = u * p
            act[rows, n:n + 256] = a.astype(BF)
            gp[rows, n:n + 256] = p + (a * (1.0 - p)) * (square * (ROOT * 0.044715 * 6.0) + 2.0 * ROOT)
        for t8 in range(width // 128):
            turned = jnp.transpose(h[:, t8 * 128:t8 * 128 + 128])
            for q in range(4):
                zl, cc = (t8 % 2) * 2 + q // 2, q % 2
                first = (t8 // 2) * 128 + zl * 32
                hT[cc, first:first + 32, rows] = turned[q * 32:q * 32 + 32, :]
        return carry

    steps = points // BLK
    before = steps // 2
    lax.fori_loop(0, before, forward, 0)

    pl.semaphore_wait(barrier, len(partners))
    pred_copies = []
    for c in range(NCH):
        chunk = []
        for j in range(1, MEMBERS):
            to = (m + j) % MEMBERS
            cols = pl.ds(pl.multiple_of(c * half + 128 * to, 128), 128)
            copy = remote(pred_hbm.at[0, :, cols], prcv.at[c, m], psem.at[c], j, member_dev(to))
            copy.start()
            chunk.append(copy)
        pred_copies.append(chunk)

    lax.fori_loop(before, steps, forward, 0)

    grad_copies = []
    for c in range(NCH):
        own_copies[2 * c].wait()
        own_copies[2 * c + 1].wait()
        for copy in pred_copies[c]:
            copy.wait_recv()
        cols = pl.ds(pl.multiple_of(c * half + 128 * m, 128), 128)
        weight = vcol * area[:, cols]
        rounded = weight.astype(BF).astype(F32)
        aim = tgt[c].astype(F32)
        preds = [prcv[c, k].astype(F32) for k in range(MEMBERS)]
        counts = [None] * MEMBERS
        for i in range(MEMBERS):
            for k in range(i):
                s = jnp.where(preds[i] > preds[k], 1.0, jnp.where(preds[i] < preds[k], -1.0, 0.0))
                counts[i] = s if counts[i] is None else counts[i] + s
                counts[k] = -s if counts[k] is None else counts[k] - s
        for k in range(MEMBERS):
            s = jnp.where(preds[k] > aim, 1.0, jnp.where(preds[k] < aim, -1.0, 0.0))
            grad = weight * s / MEMBERS - (rounded * counts[k]) / (MEMBERS * (MEMBERS - 1))
            gout[c, k, :V, :] = grad.astype(BF)
        chunk = []
        for j in range(1, MEMBERS):
            to = (m + j) % MEMBERS
            copy = remote(gout.at[c, to], gbuf.at[pl.ds(0, VS), cols], gsem.at[c], j, member_dev(to))
            copy.start()
            chunk.append(copy)
        gbuf[0:VS, cols] = gout[c, m]
        grad_copies.append(chunk)

    def back(i, carry):
        rows = pl.ds(pl.multiple_of(i * 128, 128), 128)
        turned = jnp.transpose(gbuf[:, rows])
        for n in range(0, width, 512):
            pg[rows, n:n + 512] = (dot(turned, woT[:, n:n + 512]) * gp[rows, n:n + 512]).astype(BF)
        return carry

    def hg_copy(i):
        rows = pl.ds(pl.multiple_of(i * BLK, BLK), BLK)
        return pltpu.make_async_copy(hgs.at[rows], hg_hbm.at[0, rows], osem.at[i])

    def hidden_step(i, carry):
        rows = pl.ds(pl.multiple_of(i * BLK, BLK), BLK)
        for n in range(0, width, 256):
            hgs[rows, n:n + 256] = dot_nt(pg[rows, :], win[n:n + 256, :]).astype(BF)
        hg_copy(i).start()
        return carry

    per = half // BLK
    for c in range(NCH):
        for copy in grad_copies[c]:
            copy.wait_recv()
        lax.fori_loop(c * (half // 128), (c + 1) * (half // 128), back, 0)
        if c < NCH - 1:
            lax.fori_loop(c * per, (c + 1) * per, hidden_step, 0)

    other = 1 - core
    sibling = dev(x, y, z, other)


    def rows4(value, parts):
        return value.reshape((parts, value.shape[0] // parts) + value.shape[1:])

    core_copies = []
    x1, y1 = [], []
    for b in range(NWB):
        for mm in range(2):
            for n in range(0, WB, 256):
                csnd[b, mm * 256:mm * 256 + 256, n:n + 256] = dot(
                    hT[other, mm * 256:mm * 256 + 256, :], pg[:, b * WB + n:b * WB + n + 256]
                ).astype(BF)
        copy = remote(csnd.at[b], crcv.at[b], csem, b, sibling)
        copy.start()
        core_copies.append(copy)
        for mm in range(2):
            for n in range(0, WB, 256):
                own[b, 2 * mm:2 * mm + 2, :, n:n + 256] = rows4(
                    dot(hT[core, mm * 256:mm * 256 + 256, :], pg[:, b * WB + n:b * WB + n + 256]), 2
                )
        copy.wait_recv()
        for q in range(4):
            total = own[b, q] + crcv[b, q * 128:q * 128 + 128, :].astype(F32)
            own[b, q] = total
            s1[b, q] = total.astype(BF)
        for j in (1, 2, 3):
            xx, yy = (x + j) % 4, (y + j) % 4
            copy = remote(s1.at[b, xx, pl.ds(0, 64)], r1a.at[b, x], x1sem.at[b], j, dev(xx, y, z, core))
            copy.start()
            x1.append(copy)
            cols = pl.ds(pl.multiple_of(yy * 128, 128), 128)
            copy = remote(s1.at[b, :, pl.ds(64, 64), cols], r1b.at[b, y], y1sem.at[b], j, dev(x, yy, z, core))
            copy.start()
            y1.append(copy)
        if b == 0:
            for h8 in range(width // 128):
                turned = jnp.transpose(dot(gbuf[...], act[:, h8 * 128:h8 * 128 + 128]))
                for q in range(4):
                    zl, cc = (h8 % 2) * 2 + q // 2, q % 2
                    first = (h8 // 2) * 128 + zl * 32
                    oown[cc, first:first + 32, :] = turned[q * 32:q * 32 + 32, :]
            cosnd[...] = oown[other].astype(BF)
            ocopy = remote(cosnd, corcv, csem, NWB, sibling)
            ocopy.start()
            core_copies.append(ocopy)
    ocopy.wait_recv()
    total = oown[core] + corcv[...].astype(F32)
    oown[core] = total
    s1o[...] = rows4(total.astype(BF), 4)
    o1 = []
    for j in (1, 2, 3):
        xx = (x + j) % 4
        copy = remote(s1o.at[xx], r1o.at[x], o1sem, j, dev(xx, y, z, core))
        copy.start()
        o1.append(copy)

    lax.fori_loop((NCH - 1) * per, NCH * per, hidden_step, 0)

    own_cols = pl.ds(pl.multiple_of(y * 128, 128), 128)
    for copy in x1 + y1 + o1:
        copy.wait_recv()
    for b in range(NWB):
        ta = own[b, x, 0:64, :]
        tb = own[b, :, 64:128, own_cols]
        for j in (1, 2, 3):
            ta = ta + r1a[b, (x + j) % 4].astype(F32)
            tb = tb + r1b[b, (y + j) % 4].astype(F32)
        a2[b] = ta
        b2[b] = tb
        for q in range(4):
            s2a[q, 64 * b:64 * b + 64, :] = ta[:, q * 128:q * 128 + 128].astype(BF)
            s2b[q, 64 * b:64 * b + 64, :] = tb[q].astype(BF)
    to = oown[core, pl.ds(pl.multiple_of(x * 128, 128), 128), :]
    for j in (1, 2, 3):
        to = to + r1o[(x + j) % 4].astype(F32)
    oown[core, pl.ds(pl.multiple_of(x * 128, 128), 128), :] = to
    for q in range(4):
        s2a[q, 128:160, :] = to[q * 32:q * 32 + 32, :].astype(BF)
    second = []
    for j in (1, 2, 3):
        xx, yy = (x + j) % 4, (y + j) % 4
        copy = remote(s2a.at[yy], r2a.at[y], a2sem, j, dev(x, yy, z, core))
        copy.start()
        second.append(copy)
        copy = remote(s2b.at[xx], r2b.at[x], b2sem, j, dev(xx, y, z, core))
        copy.start()
        second.append(copy)
    for copy in second:
        copy.wait_recv()

    for b in range(NWB):
        ta = a2[b, :, own_cols]
        tb = b2[b, x]
        for j in (1, 2, 3):
            ta = ta + r2a[(y + j) % 4, 64 * b:64 * b + 64, :].astype(F32)
            tb = tb + r2b[(x + j) % 4, 64 * b:64 * b + 64, :].astype(F32)
        s4[0:64, :] = ta
        s4[64:128, :] = tb
        for q in range(4):
            r4[q, 32 * b:32 * b + 32, :] = s4[q * 32:q * 32 + 32, :]
            s3[q, 32 * b:32 * b + 32, :] = s4[q * 32:q * 32 + 32, :].astype(BF)
    to = oown[core, pl.ds(pl.multiple_of(x * 128 + y * 32, 32), 32), :]
    for j in (1, 2, 3):
        to = to + r2a[(y + j) % 4, 128:160, :].astype(F32)
    for q in range(4):
        s3[q, 64:96, :] = to.astype(BF)
    third = []
    for j in range(1, 8):
        zz = (z + j) % 8
        copy = remote(s3.at[zz % 4], r3.at[z], z3sem, j, dev(x, y, zz, core))
        copy.start()
        third.append(copy)
    mine = r4[z_lo, 0:64, :]
    total = jnp.concatenate([mine, to], axis=0)
    for copy in third:
        copy.wait_recv()
    for j in range(1, 8):
        total = total + r3[(z + j) % 8].astype(F32)
    total = total * scale
    s4[0:96, :] = total

    fourth = []
    for j in (1, 2, 3):
        yy = (y + j) % 4
        copy = remote(s4.at[pl.ds(0, 96)], r5(r4).at[y], y4sem, j, dev(x, yy, z, core))
        copy.start()
        fourth.append(copy)
    r4[4 + y] = total
    for copy in fourth:
        copy.wait_recv()
    for q in range(4):
        for b in range(NWB):
            win_out[:, b * WB + q * 128:b * WB + q * 128 + 128] = r4[4 + q, 32 * b:32 * b + 32, :]
    wout_out[...] = r4[4 + z_lo, 64:96, 0:V]

    for chunk in pred_copies + grad_copies:
        for copy in chunk:
            copy.wait_send()
    for copy in core_copies + x1 + y1 + o1 + second + third + fourth:
        copy.wait_send()

    def drain(i, carry):
        hg_copy(i).wait()
        return carry

    lax.fori_loop(0, steps, drain, 0)


def r5(ref):
    return ref.at[pl.ds(4, 4)]


def shards(hidden, pred, target, area, var_weight, w_in, w_out):
    points, width = hidden.shape[1:]
    scale = 1.0 / math.sqrt(points * lax.axis_size("grid") * MEMBERS)
    share = width // lax.axis_size("grid")
    any_spec = pl.BlockSpec(memory_space=pl.ANY)
    vmem_spec = pl.BlockSpec(memory_space=pltpu.VMEM)

    def vm(*shape, dtype=BF):
        return pltpu.VMEM(shape, dtype)

    def sems(*shape):
        return pltpu.SemaphoreType.DMA(shape)

    return pl.pallas_call(
        functools.partial(kernel, scale),
        out_shape=(
            jax.ShapeDtypeStruct(hidden.shape, BF),
            jax.ShapeDtypeStruct((share, width), F32),
            jax.ShapeDtypeStruct((share, V), F32),
        ),
        in_specs=[any_spec, any_spec, any_spec, vmem_spec, vmem_spec, any_spec, vmem_spec],
        out_specs=(any_spec, vmem_spec, vmem_spec),
        scratch_shapes=[
            vm(points, width), vm(width, width), vm(2, width // 2, points), vm(points, width),
            vm(points, width, dtype=F32), vm(points, width), vm(points, width), vm(width, VP), vm(VP, width),
            vm(NCH, MEMBERS, V, 128), vm(NCH, V, 128), vm(NCH, MEMBERS, VS, 128), vm(VP, points),
            vm(NWB, width // 2, WB), vm(NWB, width // 2, WB), vm(NWB, 4, 128, WB, dtype=F32),
            vm(width // 2, VP), vm(width // 2, VP), vm(2, width // 2, VP, dtype=F32),
            vm(NWB, 4, 128, WB), vm(4, 128, VP), vm(NWB, 4, 64, WB), vm(NWB, 4, 4, 64, 128), vm(4, 128, VP),
            vm(NWB, 64, WB, dtype=F32), vm(NWB, 4, 64, 128, dtype=F32),
            vm(4, 160, 128), vm(4, 128, 128), vm(4, 160, 128), vm(4, 128, 128),
            vm(4, 96, 128), vm(8, 96, 128), vm(128, 128, dtype=F32), vm(8, 96, 128, dtype=F32),
            sems(1 + 2 * NCH), sems(points // BLK), sems(points // BLK),
            sems(NCH, 2, MEMBERS), sems(NCH, 2, MEMBERS), sems(2, NWB + 1),
            sems(NWB, 2, 4), sems(NWB, 2, 4), sems(2, 4), sems(2, 4), sems(2, 4), sems(2, 8), sems(2, 4),
        ],
        compiler_params=pltpu.CompilerParams(
            collective_id=0, has_side_effects=True, vmem_limit_bytes=60 * 1024 * 1024
        ),
    )(hidden, pred, target, area.reshape(1, -1), var_weight.reshape(1, -1), w_in, w_out)


def solution(mesh):
    return jax.shard_map(
        shards,
        mesh=mesh,
        in_specs=(
            P("member", "grid", None),
            P("member", None, "grid"),
            P(None, "grid"),
            P("grid"),
            P(),
            P(),
            P(),
        ),
        out_specs=(P("member", "grid", None), P("grid", None), P("grid", None)),
        check_vma=False,
    )
```

time: 401 us -> 82.6 us (0.21)
  waiting for transfers between devices: 326 us -> 0 us
  Pallas kernels: 0 us -> 74.1 us
  matrix products: 30.9 us -> 0 us
  starting transfers between devices: 18 us -> 0 us
  between operations: 14.2 us -> 0.66 us
  other arithmetic: 5.64 us -> 0 us
  local copies, waits for them, and re-layouts: 2.83 us -> 7.73 us
    psum x1 -> x0, waiting for transfers between devices: 262 us -> none  [shards(): in_sum, out_sum = lax.psum((in_term, out_term), ('member', 'grid'))]
    pallas_call x0 -> x1, Pallas kernels: none -> 74.1 us  [shards(): pl.pallas_call(functools.partial(kernel, scale), out_shape=(jax.ShapeDtyp...]
    ppermute x7 -> x0, waiting for transfers between devices: 63.8 us -> none  [shifted(): return lax.ppermute(value, axis, pairs)]
    dot_general x5 -> x0, matrix products: 30.9 us -> none  [the longest x1 8.31 us: shards(): lax.dot_general(pre_grad, w_in, (((1,), (1,)), ((), ())), preferred_eleme...]
    ppermute x7 -> x0, starting transfers between devices: 18 us -> none  [shifted(): return lax.ppermute(value, axis, pairs)]
    unnamed x17 -> x8, local copies, waits for them, and re-layouts: 2.83 us -> 7.73 us
  transfers between devices with their start and end apart: 8 -> 0, of which waited for: 6 -> 0; matrix products, arithmetic and copies ran while one was open for 4% -> 0% of each run, Pallas kernels for 0% -> 0%
where the time goes in v1:
time: 82.6 us; the launch traced here: 82.5 us
  Pallas kernels  74.1 us (90%)
  local copies, waits for them, and re-layouts  7.73 us (9%)
    pallas_call x1, Pallas kernels, shards(): pl.pallas_call(functools.partial(kernel, scale), out_shape=(jax.ShapeDtyp...  74.1 us
    unnamed x8, local copies, waits for them, and re-layouts  7.73 us

profile of v1, /device:TPU:32, one launch (start us, length us, event | category | flops | bytes accessed | tf_op | source)
XLA Modules:
  0.0 82.5 jit_solution(16345457176051623820)
XLA Ops:
  0.6 1.8 %copy.10.wout = bf16[1024,100]{1,0:T(8,128)(2,1)} copy(bf16[1024,100]{0,1:T(8,128)(2,1)} %param.13) | data formatting | bytes 409600 | tf_op args[6]
  2.4 74.1 %shard_map.94 = (bf16[1,2048,1024]{2,1,0:T(8,128)(2,1)}, f32[32,1024]{1,0:T(8,128)}, f32[32,100]{1,0:T(8,128)}) custom-call(bf16[1,2048,1024]{2,1,0:T(8,128)(2,1)} %hid_hbm.1, bf16[1,100,2048]{2,1,0:T(8,128)(2,1)} %pred_hbm.1, bf16[100,2048]{1,0:T(8,128)(2,1)} %tgt_hbm.1, f32[1,2048]{1,0:T(1,128)} %bitcast.2, f32[1,100]{1,0:T(1,128)} %bitcast.3, ...), custom_call_target="tpu_custom_call" | custom-call | tf_op jit(solution)/shard_map/pallas_call | solution.py:362
  76.5 0.0 copy-start
  76.5 0.0 copy-start.1
  76.5 4.7 %copy.14 = bf16[1,2048,1024]{2,1,0:T(8,128)(2,1)} copy(bf16[1,2048,1024]{2,1,0:T(8,128)(2,1)} %get-tuple-element.6) | data formatting | bytes 8388608
  81.2 0.0 copy-done
  81.2 0.7 copy.15
  81.9 0.0 copy-done.1
  81.9 0.6 copy.16
Async XLA Ops:
  76.5 4.7 %copy-start = (f32[32,1024]{1,0:T(8,128)S(1)}, f32[32,1024]{1,0:T(8,128)}, u32[]{:S(2)}) copy-start(f32[32,1024]{1,0:T(8,128)} %get-tuple-element.7) | copy-start | bytes 393220
  76.5 5.3 %copy-start.1 = (f32[32,100]{1,0:T(8,128)S(1)}, f32[32,100]{1,0:T(8,128)}, u32[]{:S(2)}) copy-start(f32[32,100]{1,0:T(8,128)} %get-tuple-element.8) | copy-start | bytes 38404

commit v2 on v1

v2 whole, which is shorter than its diff:
```python
import functools
import math

import jax
import jax.numpy as jnp
from jax import lax
from jax.experimental import pallas as pl
from jax.experimental.pallas import tpu as pltpu
from jax.sharding import PartitionSpec as P

BF = jnp.bfloat16
F32 = jnp.float32
MEMBERS = 8
V = 100
VS = 112
VP = 128
NCH = 2
BLK = 256
WB = 512
NWB = 2
ROOT = math.sqrt(2.0 / math.pi)


def dot(a, b):
    return jnp.dot(a, b, preferred_element_type=F32)


def dot_nt(a, b):
    return lax.dot_general(a, b, (((1,), (1,)), ((), ())), preferred_element_type=F32)


def kernel(
    scale,
    hid_hbm, pred_hbm, tgt_hbm, area, vw, win_hbm, wout_t,
    hgs, win_out, wout_out,
    hid, win, hT, act, gp, pg, woT,
    psrc, prcv, tgt, gout, gbuf,
    acc, csnd, crcv, oacc, cosnd, corcv, oown,
    s1, s1o, r1a, r1b, r1o, a2, b2,
    s2a, s2b, r2a, r2b, z4, s3, r3, s4, r4,
    lsem, hsem, psem, gsem, csem, x1sem, y1sem, o1sem, a2sem, b2sem, z3sem, y4sem,
):
    points = hid.shape[0]
    width = hid.shape[1]
    half = points // NCH
    m = lax.axis_index("member")
    g = lax.axis_index("grid")
    y, z_hi = m // 2, m % 2
    x, z_lo, core = g // 8, (g // 2) % 4, g % 2
    z = z_hi * 4 + z_lo

    def dev(xx, yy, zz, cc):
        return (yy * 2 + zz // 4, (xx * 4 + zz % 4) * 2 + cc)

    def member_dev(mm):
        return (mm, g)

    def remote(src, dst, sems, j, target):
        return pltpu.make_async_remote_copy(
            src_ref=src, dst_ref=dst, send_sem=sems.at[0, j], recv_sem=sems.at[1, j],
            device_id=target, device_id_type=pl.DeviceIdType.MESH,
        )

    barrier = pltpu.get_barrier_semaphore()
    partners = [member_dev((m + j) % MEMBERS) for j in range(1, MEMBERS)]
    partners += [dev(x, y, (z + j) % 8, core) for j in (1, 2, 3, 5, 6, 7)]
    partners += [dev((x + j) % 4, y, z, core) for j in (1, 2, 3)]
    partners += [dev(x, y, z, 1 - core)]
    for partner in partners:
        pl.semaphore_signal(barrier, inc=1, device_id=partner, device_id_type=pl.DeviceIdType.MESH)

    win_copy = pltpu.make_async_copy(win_hbm, win, lsem.at[0, 0])
    win_copy.start()

    def hid_copy(i):
        rows = pl.ds(pl.multiple_of(i * BLK, BLK), BLK)
        return pltpu.make_async_copy(hid_hbm.at[0, rows], hid.at[rows], hsem.at[i])

    own_copies, source_copies = [], []
    for c in range(NCH):
        mine = pl.ds(pl.multiple_of(c * half + 128 * m, 128), 128)
        own_copies.append(pltpu.make_async_copy(pred_hbm.at[0, :, mine], prcv.at[c, m], lsem.at[1, c]))
        own_copies.append(pltpu.make_async_copy(tgt_hbm.at[:, mine], tgt.at[c], lsem.at[2, c]))
        for k in range(MEMBERS):
            cols = pl.ds(c * half + 128 * k, 128)
            source_copies.append(pltpu.make_async_copy(pred_hbm.at[0, :, cols], psrc.at[c, k], lsem.at[3 + k, c]))
    for copy in source_copies + own_copies:
        copy.start()
    hid_copy(0).start()
    for i in range(1, points // BLK):
        hid_copy(i).start()


    def forward(i, carry):
        hid_copy(i).wait()
        rows = pl.ds(pl.multiple_of(i * BLK, BLK), BLK)
        h = hid[rows, :]
        for n in range(0, width, 256):
            u = dot(h, win[:, n:n + 256])
            square = u * u
            t = jnp.tanh(u * (square * (ROOT * 0.044715) + ROOT))
            p = 0.5 * t + 0.5
            a = u * p
            act[rows, n:n + 256] = a.astype(BF)
            gp[rows, n:n + 256] = p + (a * (1.0 - p)) * (square * (ROOT * 0.044715 * 6.0) + 2.0 * ROOT)
        for t8 in range(width // 128):
            turned = jnp.transpose(h[:, t8 * 128:t8 * 128 + 128])
            for q in range(4):
                zl, cc = (t8 % 2) * 2 + q // 2, q % 2
                first = (t8 // 2) * 128 + zl * 32
                hT[cc, first:first + 32, rows] = turned[q * 32:q * 32 + 32, :]
        return carry

    steps = points // BLK

    for copy in source_copies:
        copy.wait()
    pl.semaphore_wait(barrier, len(partners))
    pred_copies = []
    for c in range(NCH):
        chunk = []
        for j in range(1, MEMBERS):
            to = (m + j) % MEMBERS
            copy = remote(psrc.at[c, to], prcv.at[c, m], psem.at[c], j, member_dev(to))
            copy.start()
            chunk.append(copy)
        pred_copies.append(chunk)

    gbuf[:, VS:VP, :] = jnp.zeros((NCH * MEMBERS, VP - VS, 128), BF)
    gout[...] = jnp.zeros_like(gout)
    woT[...] = jnp.zeros_like(woT)
    woT[0:V, :] = wout_t[...]
    rows_at = lax.broadcasted_iota(jnp.int32, (V, V), 0)
    cols_at = lax.broadcasted_iota(jnp.int32, (V, V), 1)
    vcol = jnp.sum(jnp.where(rows_at == cols_at, jnp.broadcast_to(vw[...], (V, V)), 0.0), axis=1, keepdims=True)
    win_copy.wait()
    lax.fori_loop(0, steps, forward, 0)

    grad_copies = []
    for c in range(NCH):
        own_copies[2 * c].wait()
        own_copies[2 * c + 1].wait()
        for copy in pred_copies[c]:
            copy.wait_recv()
        cols = pl.ds(pl.multiple_of(c * half + 128 * m, 128), 128)
        weight = vcol * area[:, cols]
        rounded = weight.astype(BF).astype(F32)
        aim = tgt[c].astype(F32)
        preds = [prcv[c, k].astype(F32) for k in range(MEMBERS)]
        counts = [None] * MEMBERS
        for i in range(MEMBERS):
            for k in range(i):
                s = jnp.where(preds[i] > preds[k], 1.0, jnp.where(preds[i] < preds[k], -1.0, 0.0))
                counts[i] = s if counts[i] is None else counts[i] + s
                counts[k] = -s if counts[k] is None else counts[k] - s
        for k in range(MEMBERS):
            s = jnp.where(preds[k] > aim, 1.0, jnp.where(preds[k] < aim, -1.0, 0.0))
            grad = weight * s / MEMBERS - (rounded * counts[k]) / (MEMBERS * (MEMBERS - 1))
            gout[c, k, :V, :] = grad.astype(BF)
        chunk = []
        for j in range(1, MEMBERS):
            to = (m + j) % MEMBERS
            copy = remote(gout.at[c, to], gbuf.at[c * MEMBERS + m, pl.ds(0, VS)], gsem.at[c], j, member_dev(to))
            copy.start()
            chunk.append(copy)
        gbuf[c * MEMBERS + m, 0:VS, :] = gout[c, m]
        grad_copies.append(chunk)

    def back(i, carry):
        rows = pl.ds(pl.multiple_of(i * 128, 128), 128)
        turned = jnp.transpose(gbuf[i])
        for n in range(0, width, 512):
            pg[rows, n:n + 512] = (dot(turned, woT[:, n:n + 512]) * gp[rows, n:n + 512]).astype(BF)
        return carry

    def hidden_step(i, carry):
        rows = pl.ds(pl.multiple_of(i * BLK, BLK), BLK)
        for n in range(0, width, 256):
            hgs[0, rows, n:n + 256] = dot_nt(pg[rows, :], win[n:n + 256, :]).astype(BF)
        return carry

    other = 1 - core
    sibling = dev(x, y, z, other)
    last = NCH - 1

    def in_tiles(c, which, b):
        for mm in range(0, width // 2, 256):
            for n in range(0, WB, 256):
                yield mm, n, dot(
                    hT[which, mm:mm + 256, c * half:(c + 1) * half],
                    pg[c * half:(c + 1) * half, b * WB + n:b * WB + n + 256],
                )

    def out_rows(c):
        blocks = [gbuf[c * MEMBERS + k] for k in range(MEMBERS)]
        return dot(jnp.concatenate(blocks, axis=1), act[c * half:(c + 1) * half, :])

    for c in range(NCH):
        for copy in grad_copies[c]:
            copy.wait_recv()
        lax.fori_loop(c * MEMBERS, (c + 1) * MEMBERS, back, 0)
        if c == last:
            break
        for which in range(2):
            for b in range(NWB):
                for mm, n, value in in_tiles(c, which, b):
                    if c > 0:
                        value = value + acc[which, b, mm:mm + 256, n:n + 256]
                    acc[which, b, mm:mm + 256, n:n + 256] = value
        oacc[...] = out_rows(c) if c == 0 else oacc[...] + out_rows(c)

    core_copies = []
    for b in range(NWB):
        for mm, n, value in in_tiles(last, other, b):
            value = value + acc[other, b, mm:mm + 256, n:n + 256]
            csnd[b, mm:mm + 256, n:n + 256] = value.astype(BF)
        copy = remote(csnd.at[b], crcv.at[b], csem, b, sibling)
        copy.start()
        core_copies.append(copy)
    out_term = oacc[...] + out_rows(last)
    for h8 in range(width // 128):
        turned = jnp.transpose(out_term[:, h8 * 128:h8 * 128 + 128])
        for q in range(4):
            zl, cc = (h8 % 2) * 2 + q // 2, q % 2
            first = (h8 // 2) * 128 + zl * 32
            oown[cc, first:first + 32, :] = turned[q * 32:q * 32 + 32, :]
    cosnd[...] = oown[other].astype(BF)
    copy = remote(cosnd, corcv, csem, NWB, sibling)
    copy.start()
    core_copies.append(copy)

    x1, y1, o1 = [], [], []
    for b in range(NWB):
        for mm, n, value in in_tiles(last, core, b):
            acc[core, b, mm:mm + 256, n:n + 256] = value + acc[core, b, mm:mm + 256, n:n + 256]
        core_copies[b].wait_recv()
        for q in range(4):
            rows = slice(q * 128, q * 128 + 128)
            total = acc[core, b, rows, :] + crcv[b, rows, :].astype(F32)
            acc[core, b, rows, :] = total
            s1[b, q] = total.astype(BF)
        for j in (1, 2, 3):
            xx, yy = (x + j) % 4, (y + j) % 4
            copy = remote(s1.at[b, xx, pl.ds(0, 64)], r1a.at[b, x], x1sem.at[b], j, dev(xx, y, z, core))
            copy.start()
            x1.append(copy)
            cols = pl.ds(pl.multiple_of(yy * 128, 128), 128)
            copy = remote(s1.at[b, :, pl.ds(64, 64), cols], r1b.at[b, y], y1sem.at[b], j, dev(x, yy, z, core))
            copy.start()
            y1.append(copy)
    core_copies[NWB].wait_recv()
    for q in range(4):
        rows = slice(q * 128, q * 128 + 128)
        total = oown[core, rows, :] + corcv[rows, :].astype(F32)
        oown[core, rows, :] = total
        s1o[q] = total.astype(BF)
    for j in (1, 2, 3):
        xx = (x + j) % 4
        copy = remote(s1o.at[xx], r1o.at[x], o1sem, j, dev(xx, y, z, core))
        copy.start()
        o1.append(copy)

    per = steps // 2
    lax.fori_loop(0, per, hidden_step, 0)

    own_cols = pl.ds(pl.multiple_of(y * 128, 128), 128)
    own_x = pl.multiple_of(x * 128, 128)
    for copy in x1 + y1 + o1:
        copy.wait_recv()
    for b in range(NWB):
        ta = acc[core, b, pl.ds(own_x, 64), :]
        for j in (1, 2, 3):
            ta = ta + r1a[b, (x + j) % 4].astype(F32)
        a2[b] = ta
        for q in range(4):
            tb = acc[core, b, q * 128 + 64:q * 128 + 128, own_cols]
            for j in (1, 2, 3):
                tb = tb + r1b[b, (y + j) % 4, q].astype(F32)
            b2[b, q] = tb
            s2a[q, 64 * b:64 * b + 64, :] = ta[:, q * 128:q * 128 + 128].astype(BF)
            s2b[q, 64 * b:64 * b + 64, :] = tb.astype(BF)
    to = oown[core, pl.ds(own_x, 128), :]
    for j in (1, 2, 3):
        to = to + r1o[(x + j) % 4].astype(F32)
    for q in range(4):
        part = jnp.concatenate([to[zl * 32 + q * 8:zl * 32 + q * 8 + 8, :] for zl in range(4)], axis=0)
        oown[core, q * 32:q * 32 + 32, :] = part
        s2a[q, 128:160, :] = part.astype(BF)
    second = []
    for j in (1, 2, 3):
        xx, yy = (x + j) % 4, (y + j) % 4
        copy = remote(s2a.at[yy], r2a.at[y], a2sem, j, dev(x, yy, z, core))
        copy.start()
        second.append(copy)
        copy = remote(s2b.at[xx], r2b.at[x], b2sem, j, dev(xx, y, z, core))
        copy.start()
        second.append(copy)
    lax.fori_loop(per, steps, hidden_step, 0)
    for copy in second:
        copy.wait_recv()

    empty = jnp.zeros((8, 128), F32)
    to = oown[core, pl.ds(pl.multiple_of(y * 32, 32), 32), :]
    for j in (1, 2, 3):
        to = to + r2a[(y + j) % 4, 128:160, :].astype(F32)
    sums = []
    for b in range(NWB):
        ta = a2[b, :, own_cols]
        tb = b2[b, x]
        for j in (1, 2, 3):
            ta = ta + r2a[(y + j) % 4, 64 * b:64 * b + 64, :].astype(F32)
            tb = tb + r2b[(x + j) % 4, 64 * b:64 * b + 64, :].astype(F32)
        sums.append((ta[0:32], ta[32:64], tb[0:32], tb[32:64]))
    for q in range(4):
        part = jnp.concatenate([sums[0][q], sums[1][q], to[q * 8:q * 8 + 8, :], empty], axis=0)
        z4[q] = part
        s3[q] = part.astype(BF)
    third = []
    for j in range(1, 8):
        zz = (z + j) % 8
        copy = remote(s3.at[zz % 4], r3.at[z], z3sem, j, dev(x, y, zz, core))
        copy.start()
        third.append(copy)
    total = z4[z_lo]
    for copy in third:
        copy.wait_recv()
    for j in range(1, 8):
        total = total + r3[(z + j) % 8].astype(F32)
    total = total * scale
    s4[...] = total.astype(BF)

    fourth = []
    for j in (1, 2, 3):
        copy = remote(s4, r4.at[y], y4sem, j, dev(x, (y + j) % 4, z, core))
        copy.start()
        fourth.append(copy)
    r4[y] = s4[...]
    for chunk in pred_copies + grad_copies:
        for copy in chunk:
            copy.wait_send()
    for copy in core_copies + x1 + y1 + o1 + second + third:
        copy.wait_send()
    for copy in fourth:
        copy.wait_recv()
    for q in range(4):
        got = r4[q].astype(F32)
        for b in range(NWB):
            win_out[:, b * WB + q * 128:b * WB + q * 128 + 128] = got[32 * b:32 * b + 32, :]
        wout_out[q * 8:q * 8 + 8, :] = got[64:72, 0:V]
    for copy in fourth:
        copy.wait_send()


def place(hg_in, in_in, out_in, hg_out, in_out, out_out, sem):
    points = hg_in.shape[1]
    parts = 4
    copies = []
    for i in range(parts):
        rows = pl.ds(i * (points // parts), points // parts)
        copies.append(pltpu.make_async_copy(hg_in.at[0, rows], hg_out.at[0, rows], sem.at[i]))
    copies.append(pltpu.make_async_copy(in_in, in_out, sem.at[parts]))
    copies.append(pltpu.make_async_copy(out_in, out_out, sem.at[parts + 1]))
    for copy in copies:
        copy.start()
    for copy in copies:
        copy.wait()


def shards(hidden, pred, target, area, var_weight, w_in, w_out):
    points, width = hidden.shape[1:]
    scale = 1.0 / math.sqrt(points * lax.axis_size("grid") * MEMBERS)
    share = width // lax.axis_size("grid")
    any_spec = pl.BlockSpec(memory_space=pl.ANY)
    vmem_spec = pl.BlockSpec(memory_space=pltpu.VMEM)

    def vm(*shape, dtype=BF):
        return pltpu.VMEM(shape, dtype)

    def sems(*shape):
        return pltpu.SemaphoreType.DMA(shape)

    out_types = (
        jax.ShapeDtypeStruct(hidden.shape, BF),
        jax.ShapeDtypeStruct((share, width), F32),
        jax.ShapeDtypeStruct((share, V), F32),
    )
    half = width // 2
    results = pl.pallas_call(
        functools.partial(kernel, scale),
        out_shape=tuple(pltpu.VMEM(t.shape, t.dtype) for t in out_types),
        in_specs=[any_spec, any_spec, any_spec, vmem_spec, vmem_spec, any_spec, vmem_spec],
        out_specs=(vmem_spec, vmem_spec, vmem_spec),
        scratch_shapes=[
            vm(points, width), vm(width, width), vm(2, half, points), vm(points, width),
            vm(points, width, dtype=F32), vm(points, width), vm(VP, width),
            vm(NCH, MEMBERS, V, 128), vm(NCH, MEMBERS, V, 128), vm(NCH, V, 128), vm(NCH, MEMBERS, VS, 128),
            vm(NCH * MEMBERS, VP, 128),
            vm(2, NWB, half, WB, dtype=F32), vm(NWB, half, WB), vm(NWB, half, WB),
            vm(VP, width, dtype=F32), vm(half, VP), vm(half, VP), vm(2, half, VP, dtype=F32),
            vm(NWB, 4, 128, WB), vm(4, 128, VP), vm(NWB, 4, 64, WB), vm(NWB, 4, 4, 64, 128), vm(4, 128, VP),
            vm(NWB, 64, WB, dtype=F32), vm(NWB, 4, 64, 128, dtype=F32),
            vm(4, 160, 128), vm(4, 128, 128), vm(4, 160, 128), vm(4, 128, 128),
            vm(4, 80, 128, dtype=F32), vm(4, 80, 128), vm(8, 80, 128), vm(80, 128), vm(4, 80, 128),
            sems(3 + MEMBERS, NCH), sems(points // BLK),
            sems(NCH, 2, MEMBERS), sems(NCH, 2, MEMBERS), sems(2, NWB + 1),
            sems(NWB, 2, 4), sems(NWB, 2, 4), sems(2, 4), sems(2, 4), sems(2, 4), sems(2, 8), sems(2, 4),
        ],
        compiler_params=pltpu.CompilerParams(
            collective_id=0, has_side_effects=True, vmem_limit_bytes=50 * 1024 * 1024
        ),
    )(hidden, pred, target, area.reshape(1, -1), var_weight.reshape(1, -1), w_in, w_out.T)
    return pl.pallas_call(
        place,
        out_shape=out_types,
        in_specs=[vmem_spec] * 3,
        out_specs=(any_spec,) * 3,
        scratch_shapes=[sems(6)],
        compiler_params=pltpu.CompilerParams(vmem_limit_bytes=8 * 1024 * 1024),
    )(*results)


def solution(mesh):
    return jax.shard_map(
        shards,
        mesh=mesh,
        in_specs=(
            P("member", "grid", None),
            P("member", None, "grid"),
            P(None, "grid"),
            P("grid"),
            P(),
            P(),
            P(),
        ),
        out_specs=(P("member", "grid", None), P("grid", None), P("grid", None)),
        check_vma=False,
    )
```

time: 82.6 us -> 69.9 us (0.85)
  local copies, waits for them, and re-layouts: 7.73 us -> 0 us
  Pallas kernels: 74.1 us -> 69.2 us
    unnamed x8 -> x0, local copies, waits for them, and re-layouts: 7.73 us -> none
    pallas_call x1 -> x2, Pallas kernels: 74.1 us -> 69.2 us  [the longest x1 67.1 us: shards(): pl.pallas_call(functools.partial(kernel, scale), out_shape=tuple((pltpu.V...]
where the time goes in v2:
time: 69.9 us; the launch traced here: 69.8 us
  Pallas kernels  69.2 us (99%)
    pallas_call x1, Pallas kernels, shards(): pl.pallas_call(functools.partial(kernel, scale), out_shape=tuple((pltpu.V...  67.1 us
    pallas_call x1, Pallas kernels, shards(): pl.pallas_call(place, out_shape=out_types, in_specs=[vmem_spec] * 3, out_...  2.09 us

profile of v2, /device:TPU:32, one launch (start us, length us, event | category | flops | bytes accessed | tf_op | source)
XLA Modules:
  0.0 69.8 jit_solution(4400329356973297261)
XLA Ops:
  0.6 67.1 %shard_map.94 = (bf16[1,2048,1024]{2,1,0:T(8,128)(2,1)S(1)}, f32[32,1024]{1,0:T(8,128)S(1)}, f32[32,100]{1,0:T(8,128)S(1)}) custom-call(bf16[1,2048,1024]{2,1,0:T(8,128)(2,1)} %hid_hbm.1, bf16[1,100,2048]{2,1,0:T(8,128)(2,1)} %pred_hbm.1, bf16[100,2048]{1,0:T(8,128)(2,1)} %tgt_hbm.1, f32[1,2048]{1,0:T(1,128)} %bitcast.4, f32[1,100]{1,0:T(1,128)} %bitcast.5, ...), custom_call_target="tpu_custom_call" | custom-call | tf_op jit(solution)/shard_map/pallas_call | solution.py:388
  67.7 2.1 %shard_map.95 = (bf16[1,2048,1024]{2,1,0:T(8,128)(2,1)}, f32[32,1024]{1,0:T(8,128)}, f32[32,100]{1,0:T(8,128)}) custom-call(bf16[1,2048,1024]{2,1,0:T(8,128)(2,1)S(1)} %get-tuple-element.6.hg_in, f32[32,1024]{1,0:T(8,128)S(1)} %get-tuple-element.7.in_in, f32[32,100]{1,0:T(8,128)S(1)} %get-tuple-element.8.out_in), custom_call_target="tpu_custom_call" | custom-call | tf_op jit(solution)/shard_map/pallas_call | solution.py:412

commit v3 on v2

--- a/solution.py
+++ b/solution.py
@@ -15,7 +15,9 @@
 VS = 112
 VP = 128
 NCH = 2
-BLK = 256
+BLK = 512
+HB = 1024
+GB = 4
 WB = 512
 NWB = 2
 ROOT = math.sqrt(2.0 / math.pi)
@@ -61,9 +63,14 @@
             device_id=target, device_id_type=pl.DeviceIdType.MESH,
         )
 
+    members_far_first = [
+        (1 + k, 2 * ((y + dy) % 4) + (z_hi + dz) % 2)
+        for k, (dy, dz) in enumerate(((2, 1), (1, 1), (3, 1), (0, 1), (2, 0), (1, 0), (3, 0)))
+    ]
+
     barrier = pltpu.get_barrier_semaphore()
-    partners = [member_dev((m + j) % MEMBERS) for j in range(1, MEMBERS)]
-    partners += [dev(x, y, (z + j) % 8, core) for j in (1, 2, 3, 5, 6, 7)]
+    partners = [member_dev(to) for _, to in members_far_first]
+    partners += [dev(x, y, (z + j) % 8, core) for j in (3, 5, 2, 6, 1, 7)]
     partners += [dev((x + j) % 4, y, z, core) for j in (1, 2, 3)]
     partners += [dev(x, y, z, 1 - core)]
     for partner in partners:
@@ -119,8 +126,7 @@
     pred_copies = []
     for c in range(NCH):
         chunk = []
-        for j in range(1, MEMBERS):
-            to = (m + j) % MEMBERS
+        for j, to in members_far_first:
             copy = remote(psrc.at[c, to], prcv.at[c, m], psem.at[c], j, member_dev(to))
             copy.start()
             chunk.append(copy)
@@ -158,8 +164,7 @@
             grad = weight * s / MEMBERS - (rounded * counts[k]) / (MEMBERS * (MEMBERS - 1))
             gout[c, k, :V, :] = grad.astype(BF)
         chunk = []
-        for j in range(1, MEMBERS):
-            to = (m + j) % MEMBERS
+        for j, to in members_far_first:
             copy = remote(gout.at[c, to], gbuf.at[c * MEMBERS + m, pl.ds(0, VS)], gsem.at[c], j, member_dev(to))
             copy.start()
             chunk.append(copy)
@@ -167,14 +172,14 @@
         grad_copies.append(chunk)
 
     def back(i, carry):
-        rows = pl.ds(pl.multiple_of(i * 128, 128), 128)
-        turned = jnp.transpose(gbuf[i])
+        rows = pl.ds(pl.multiple_of(i * (GB * 128), GB * 128), GB * 128)
+        turned = jnp.concatenate([jnp.transpose(gbuf[i * GB + k]) for k in range(GB)], axis=0)
         for n in range(0, width, 512):
             pg[rows, n:n + 512] = (dot(turned, woT[:, n:n + 512]) * gp[rows, n:n + 512]).astype(BF)
         return carry
 
     def hidden_step(i, carry):
-        rows = pl.ds(pl.multiple_of(i * BLK, BLK), BLK)
+        rows = pl.ds(pl.multiple_of(i * HB, HB), HB)
         for n in range(0, width, 256):
             hgs[0, rows, n:n + 256] = dot_nt(pg[rows, :], win[n:n + 256, :]).astype(BF)
         return carry
@@ -184,12 +189,11 @@
     last = NCH - 1
 
     def in_tiles(c, which, b):
-        for mm in range(0, width // 2, 256):
-            for n in range(0, WB, 256):
-                yield mm, n, dot(
-                    hT[which, mm:mm + 256, c * half:(c + 1) * half],
-                    pg[c * half:(c + 1) * half, b * WB + n:b * WB + n + 256],
-                )
+        for n in range(0, WB, 256):
+            yield slice(n, n + 256), dot(
+                hT[which, :, c * half:(c + 1) * half],
+                pg[c * half:(c + 1) * half, b * WB + n:b * WB + n + 256],
+            )
 
     def out_rows(c):
         blocks = [gbuf[c * MEMBERS + k] for k in range(MEMBERS)]
@@ -198,41 +202,26 @@
     for c in range(NCH):
         for copy in grad_copies[c]:
             copy.wait_recv()
-        lax.fori_loop(c * MEMBERS, (c + 1) * MEMBERS, back, 0)
+        lax.fori_loop(c * (MEMBERS // GB), (c + 1) * (MEMBERS // GB), back, 0)
         if c == last:
             break
         for which in range(2):
             for b in range(NWB):
-                for mm, n, value in in_tiles(c, which, b):
-                    if c > 0:
-                        value = value + acc[which, b, mm:mm + 256, n:n + 256]
-                    acc[which, b, mm:mm + 256, n:n + 256] = value
+                for cols, value in in_tiles(c, which, b):
+                    acc[which, b, :, cols] = value if c == 0 else value + acc[which, b, :, cols]
         oacc[...] = out_rows(c) if c == 0 else oacc[...] + out_rows(c)
 
     core_copies = []
     for b in range(NWB):
-        for mm, n, value in in_tiles(last, other, b):
-            value = value + acc[other, b, mm:mm + 256, n:n + 256]
-            csnd[b, mm:mm + 256, n:n + 256] = value.astype(BF)
+        for cols, value in in_tiles(last, other, b):
+            csnd[b, :, cols] = (value + acc[other, b, :, cols]).astype(BF)
         copy = remote(csnd.at[b], crcv.at[b], csem, b, sibling)
         copy.start()
         core_copies.append(copy)
-    out_term = oacc[...] + out_rows(last)
-    for h8 in range(width // 128):
-        turned = jnp.transpose(out_term[:, h8 * 128:h8 * 128 + 128])
-        for q in range(4):
-            zl, cc = (h8 % 2) * 2 + q // 2, q % 2
-            first = (h8 // 2) * 128 + zl * 32
-            oown[cc, first:first + 32, :] = turned[q * 32:q * 32 + 32, :]
-    cosnd[...] = oown[other].astype(BF)
-    copy = remote(cosnd, corcv, csem, NWB, sibling)
-    copy.start()
-    core_copies.append(copy)
-
     x1, y1, o1 = [], [], []
     for b in range(NWB):
-        for mm, n, value in in_tiles(last, core, b):
-            acc[core, b, mm:mm + 256, n:n + 256] = value + acc[core, b, mm:mm + 256, n:n + 256]
+        for cols, value in in_tiles(last, core, b):
+            acc[core, b, :, cols] = value + acc[core, b, :, cols]
         core_copies[b].wait_recv()
         for q in range(4):
             rows = slice(q * 128, q * 128 + 128)
@@ -248,6 +237,18 @@
             copy = remote(s1.at[b, :, pl.ds(64, 64), cols], r1b.at[b, y], y1sem.at[b], j, dev(x, yy, z, core))
             copy.start()
             y1.append(copy)
+    out_term = oacc[...] + out_rows(last)
+    for h8 in range(width // 128):
+        turned = jnp.transpose(out_term[:, h8 * 128:h8 * 128 + 128])
+        for q in range(4):
+            zl, cc = (h8 % 2) * 2 + q // 2, q % 2
+            first = (h8 // 2) * 128 + zl * 32
+            oown[cc, first:first + 32, :] = turned[q * 32:q * 32 + 32, :]
+    cosnd[...] = oown[other].astype(BF)
+    copy = remote(cosnd, corcv, csem, NWB, sibling)
+    copy.start()
+    core_copies.append(copy)
+
     core_copies[NWB].wait_recv()
     for q in range(4):
         rows = slice(q * 128, q * 128 + 128)
@@ -260,7 +261,7 @@
         copy.start()
         o1.append(copy)
 
-    per = steps // 2
+    per = points // HB // 2
     lax.fori_loop(0, per, hidden_step, 0)
 
     own_cols = pl.ds(pl.multiple_of(y * 128, 128), 128)
@@ -295,7 +296,7 @@
         copy = remote(s2b.at[xx], r2b.at[x], b2sem, j, dev(xx, y, z, core))
         copy.start()
         second.append(copy)
-    lax.fori_loop(per, steps, hidden_step, 0)
+    lax.fori_loop(per, 2 * per, hidden_step, 0)
     for copy in second:
         copy.wait_recv()
 
@@ -316,7 +317,7 @@
         z4[q] = part
         s3[q] = part.astype(BF)
     third = []
-    for j in range(1, 8):
+    for j in (4, 3, 5, 2, 6, 1, 7):
         zz = (z + j) % 8
         copy = remote(s3.at[zz % 4], r3.at[z], z3sem, j, dev(x, y, zz, core))
         copy.start()
@@ -353,7 +354,7 @@
 
 def place(hg_in, in_in, out_in, hg_out, in_out, out_out, sem):
     points = hg_in.shape[1]
-    parts = 4
+    parts = 8
     copies = []
     for i in range(parts):
         rows = pl.ds(i * (points // parts), points // parts)
@@ -414,7 +415,7 @@
         out_shape=out_types,
         in_specs=[vmem_spec] * 3,
         out_specs=(any_spec,) * 3,
-        scratch_shapes=[sems(6)],
+        scratch_shapes=[sems(10)],
         compiler_params=pltpu.CompilerParams(vmem_limit_bytes=8 * 1024 * 1024),
     )(*results)
 

time: 69.9 us -> 67 us (0.959)
  Pallas kernels: 69.2 us -> 66.2 us
    pallas_call x1, Pallas kernels: 67.1 us -> 64.1 us  [shards(): pl.pallas_call(functools.partial(kernel, scale), out_shape=tuple((pltpu.V...]
where the time goes in v3:
time: 67 us; the launch traced here: 66.9 us
  Pallas kernels  66.2 us (99%)
    pallas_call x1, Pallas kernels, shards(): pl.pallas_call(functools.partial(kernel, scale), out_shape=tuple((pltpu.V...  64.1 us
    pallas_call x1, Pallas kernels, shards(): pl.pallas_call(place, out_shape=out_types, in_specs=[vmem_spec] * 3, out_...  2.13 us

profile of v3, /device:TPU:32, one launch (start us, length us, event | category | flops | bytes accessed | tf_op | source)
XLA Modules:
  0.0 66.9 jit_solution(11149768570121880599)
XLA Ops:
  0.6 64.1 %shard_map.94 = (bf16[1,2048,1024]{2,1,0:T(8,128)(2,1)S(1)}, f32[32,1024]{1,0:T(8,128)S(1)}, f32[32,100]{1,0:T(8,128)S(1)}) custom-call(bf16[1,2048,1024]{2,1,0:T(8,128)(2,1)} %hid_hbm.1, bf16[1,100,2048]{2,1,0:T(8,128)(2,1)} %pred_hbm.1, bf16[100,2048]{1,0:T(8,128)(2,1)} %tgt_hbm.1, f32[1,2048]{1,0:T(1,128)} %bitcast.4, f32[1,100]{1,0:T(1,128)} %bitcast.5, ...), custom_call_target="tpu_custom_call" | custom-call | tf_op jit(solution)/shard_map/pallas_call | solution.py:389
  64.7 2.1 %shard_map.95 = (bf16[1,2048,1024]{2,1,0:T(8,128)(2,1)}, f32[32,1024]{1,0:T(8,128)}, f32[32,100]{1,0:T(8,128)}) custom-call(bf16[1,2048,1024]{2,1,0:T(8,128)(2,1)S(1)} %get-tuple-element.6.hg_in, f32[32,1024]{1,0:T(8,128)S(1)} %get-tuple-element.7.in_in, f32[32,100]{1,0:T(8,128)S(1)} %get-tuple-element.8.out_in), custom_call_target="tpu_custom_call" | custom-call | tf_op jit(solution)/shard_map/pallas_call | solution.py:413

commit v4 on v3

--- a/solution.py
+++ b/solution.py
@@ -63,13 +63,16 @@
             device_id=target, device_id_type=pl.DeviceIdType.MESH,
         )
 
-    members_far_first = [
-        (1 + k, 2 * ((y + dy) % 4) + (z_hi + dz) % 2)
-        for k, (dy, dz) in enumerate(((2, 1), (1, 1), (3, 1), (0, 1), (2, 0), (1, 0), (3, 0)))
-    ]
+    mine_p = z_hi * 4 + y
+
+    members_far_first = []
+    for k, (dy, dz) in enumerate(((2, 1), (1, 1), (3, 1), (0, 1), (2, 0), (1, 0), (3, 0))):
+        to_y, to_z = (y + dy) % 4, (z_hi + dz) % 2
+        members_far_first.append((1 + k, to_z * 4 + to_y, 2 * to_y + to_z))
+    fars = 4
 
     barrier = pltpu.get_barrier_semaphore()
-    partners = [member_dev(to) for _, to in members_far_first]
+    partners = [member_dev(to) for _, _, to in members_far_first]
     partners += [dev(x, y, (z + j) % 8, core) for j in (3, 5, 2, 6, 1, 7)]
     partners += [dev((x + j) % 4, y, z, core) for j in (1, 2, 3)]
     partners += [dev(x, y, z, 1 - core)]
@@ -85,8 +88,8 @@
 
     own_copies, source_copies = [], []
     for c in range(NCH):
-        mine = pl.ds(pl.multiple_of(c * half + 128 * m, 128), 128)
-        own_copies.append(pltpu.make_async_copy(pred_hbm.at[0, :, mine], prcv.at[c, m], lsem.at[1, c]))
+        mine = pl.ds(pl.multiple_of(c * half + 128 * mine_p, 128), 128)
+        own_copies.append(pltpu.make_async_copy(pred_hbm.at[0, :, mine], prcv.at[c, mine_p], lsem.at[1, c]))
         own_copies.append(pltpu.make_async_copy(tgt_hbm.at[:, mine], tgt.at[c], lsem.at[2, c]))
         for k in range(MEMBERS):
             cols = pl.ds(c * half + 128 * k, 128)
@@ -126,8 +129,8 @@
     pred_copies = []
     for c in range(NCH):
         chunk = []
-        for j, to in members_far_first:
-            copy = remote(psrc.at[c, to], prcv.at[c, m], psem.at[c], j, member_dev(to))
+        for j, p, to in members_far_first:
+            copy = remote(psrc.at[c, p], prcv.at[c, mine_p], psem.at[c], j, member_dev(to))
             copy.start()
             chunk.append(copy)
         pred_copies.append(chunk)
@@ -148,7 +151,7 @@
         own_copies[2 * c + 1].wait()
         for copy in pred_copies[c]:
             copy.wait_recv()
-        cols = pl.ds(pl.multiple_of(c * half + 128 * m, 128), 128)
+        cols = pl.ds(pl.multiple_of(c * half + 128 * mine_p, 128), 128)
         weight = vcol * area[:, cols]
         rounded = weight.astype(BF).astype(F32)
         aim = tgt[c].astype(F32)
@@ -164,11 +167,11 @@
             grad = weight * s / MEMBERS - (rounded * counts[k]) / (MEMBERS * (MEMBERS - 1))
             gout[c, k, :V, :] = grad.astype(BF)
         chunk = []
-        for j, to in members_far_first:
-            copy = remote(gout.at[c, to], gbuf.at[c * MEMBERS + m, pl.ds(0, VS)], gsem.at[c], j, member_dev(to))
+        for j, p, to in members_far_first:
+            copy = remote(gout.at[c, p], gbuf.at[c * MEMBERS + mine_p, pl.ds(0, VS)], gsem.at[c], j, member_dev(to))
             copy.start()
             chunk.append(copy)
-        gbuf[c * MEMBERS + m, 0:VS, :] = gout[c, m]
+        gbuf[c * MEMBERS + mine_p, 0:VS, :] = gout[c, mine_p]
         grad_copies.append(chunk)
 
     def back(i, carry):
@@ -188,39 +191,52 @@
     sibling = dev(x, y, z, other)
     last = NCH - 1
 
-    def in_tiles(c, which, b):
+    group = GB * 128
+
+    def in_tiles(at, which, b):
+        rows = pl.ds(*at)
         for n in range(0, WB, 256):
-            yield slice(n, n + 256), dot(
-                hT[which, :, c * half:(c + 1) * half],
-                pg[c * half:(c + 1) * half, b * WB + n:b * WB + n + 256],
-            )
-
-    def out_rows(c):
-        blocks = [gbuf[c * MEMBERS + k] for k in range(MEMBERS)]
-        return dot(jnp.concatenate(blocks, axis=1), act[c * half:(c + 1) * half, :])
-
-    for c in range(NCH):
+            yield slice(n, n + 256), dot(hT[which, :, rows], pg[rows, b * WB + n:b * WB + n + 256])
+
+    def out_rows(at, first):
+        blocks = [gbuf[first + k] for k in range(at[1] // 128)]
+        return dot(jnp.concatenate(blocks, axis=1), act[pl.ds(*at), :])
+
+    def add_terms(at, first, start):
+        for which in range(2):
+            for b in range(NWB):
+                for cols, value in in_tiles(at, which, b):
+                    acc[which, b, :, cols] = value if start else value + acc[which, b, :, cols]
+        oacc[...] = out_rows(at, first) if start else oacc[...] + out_rows(at, first)
+
+    for c in range(last):
         for copy in grad_copies[c]:
             copy.wait_recv()
-        lax.fori_loop(c * (MEMBERS // GB), (c + 1) * (MEMBERS // GB), back, 0)
-        if c == last:
-            break
-        for which in range(2):
-            for b in range(NWB):
-                for cols, value in in_tiles(c, which, b):
-                    acc[which, b, :, cols] = value if c == 0 else value + acc[which, b, :, cols]
-        oacc[...] = out_rows(c) if c == 0 else oacc[...] + out_rows(c)
+        for i in range(MEMBERS // GB):
+            back(c * (MEMBERS // GB) + i, 0)
+        add_terms((c * half, half), c * MEMBERS, c == 0)
+
+    for copy in grad_copies[last][fars:]:
+        copy.wait_recv()
+    near = last * 2 + z_hi
+    back(near, 0)
+    add_terms((pl.multiple_of(near * group, group), group), near * GB, False)
+    for copy in grad_copies[last][:fars]:
+        copy.wait_recv()
+    far = last * 2 + 1 - z_hi
+    far_at = (pl.multiple_of(far * group, group), group)
+    back(far, 0)
 
     core_copies = []
     for b in range(NWB):
-        for cols, value in in_tiles(last, other, b):
+        for cols, value in in_tiles(far_at, other, b):
             csnd[b, :, cols] = (value + acc[other, b, :, cols]).astype(BF)
         copy = remote(csnd.at[b], crcv.at[b], csem, b, sibling)
         copy.start()
         core_copies.append(copy)
     x1, y1, o1 = [], [], []
     for b in range(NWB):
-        for cols, value in in_tiles(last, core, b):
+        for cols, value in in_tiles(far_at, core, b):
             acc[core, b, :, cols] = value + acc[core, b, :, cols]
         core_copies[b].wait_recv()
         for q in range(4):
@@ -237,7 +253,7 @@
             copy = remote(s1.at[b, :, pl.ds(64, 64), cols], r1b.at[b, y], y1sem.at[b], j, dev(x, yy, z, core))
             copy.start()
             y1.append(copy)
-    out_term = oacc[...] + out_rows(last)
+    out_term = oacc[...] + out_rows(far_at, far * GB)
     for h8 in range(width // 128):
         turned = jnp.transpose(out_term[:, h8 * 128:h8 * 128 + 128])
         for q in range(4):

time: 67 us -> 67.1 us (level)
  no operation moved by 1% of the time
where the time goes in v4:
time: 67.1 us; the launch traced here: 67 us
  Pallas kernels  66.2 us (99%)
  between operations  0.8 us (1%)
    pallas_call x1, Pallas kernels, shards(): pl.pallas_call(functools.partial(kernel, scale), out_shape=tuple((pltpu.V...  64.1 us
    pallas_call x1, Pallas kernels, shards(): pl.pallas_call(place, out_shape=out_types, in_specs=[vmem_spec] * 3, out_...  2.13 us

profile of v4, /device:TPU:32, one launch (start us, length us, event | category | flops | bytes accessed | tf_op | source)
XLA Modules:
  0.0 67.0 jit_solution(778332400740155078)
XLA Ops:
  0.6 64.1 %shard_map.94 = (bf16[1,2048,1024]{2,1,0:T(8,128)(2,1)S(1)}, f32[32,1024]{1,0:T(8,128)S(1)}, f32[32,100]{1,0:T(8,128)S(1)}) custom-call(bf16[1,2048,1024]{2,1,0:T(8,128)(2,1)} %hid_hbm.1, bf16[1,100,2048]{2,1,0:T(8,128)(2,1)} %pred_hbm.1, bf16[100,2048]{1,0:T(8,128)(2,1)} %tgt_hbm.1, f32[1,2048]{1,0:T(1,128)} %bitcast.4, f32[1,100]{1,0:T(1,128)} %bitcast.5, ...), custom_call_target="tpu_custom_call" | custom-call | tf_op jit(solution)/shard_map/pallas_call | solution.py:405
  64.7 2.1 %shard_map.95 = (bf16[1,2048,1024]{2,1,0:T(8,128)(2,1)}, f32[32,1024]{1,0:T(8,128)}, f32[32,100]{1,0:T(8,128)}) custom-call(bf16[1,2048,1024]{2,1,0:T(8,128)(2,1)S(1)} %get-tuple-element.6.hg_in, f32[32,1024]{1,0:T(8,128)S(1)} %get-tuple-element.7.in_in, f32[32,100]{1,0:T(8,128)S(1)} %get-tuple-element.8.out_in), custom_call_target="tpu_custom_call" | custom-call | tf_op jit(solution)/shard_map/pallas_call | solution.py:429

commit v5 on v4

--- a/solution.py
+++ b/solution.py
@@ -33,14 +33,14 @@
 
 def kernel(
     scale,
-    hid_hbm, pred_hbm, tgt_hbm, area, vw, win_hbm, wout_t,
+    hid_hbm, pred_hbm, tgt_hbm, area_hbm, vw_hbm, win_hbm, wout_hbm,
     hgs, win_out, wout_out,
-    hid, win, hT, act, gp, pg, woT,
+    area, vw, wout_t, hid, win, hT, act, gp, pg, woT,
     psrc, prcv, tgt, gout, gbuf,
     acc, csnd, crcv, oacc, cosnd, corcv, oown,
-    s1, s1o, r1a, r1b, r1o, a2, b2,
+    s1a, s1b, r1a, r1b, a2, b2,
     s2a, s2b, r2a, r2b, z4, s3, r3, s4, r4,
-    lsem, hsem, psem, gsem, csem, x1sem, y1sem, o1sem, a2sem, b2sem, z3sem, y4sem,
+    lsem, hsem, psem, gsem, csem, x1sem, y1sem, a2sem, b2sem, z3sem, y4sem,
 ):
     points = hid.shape[0]
     width = hid.shape[1]
@@ -81,6 +81,12 @@
 
     win_copy = pltpu.make_async_copy(win_hbm, win, lsem.at[0, 0])
     win_copy.start()
+    small_copies = [
+        pltpu.make_async_copy(source, target, lsem.at[0, 1 + i])
+        for i, (source, target) in enumerate(((area_hbm, area), (vw_hbm, vw), (wout_hbm, wout_t)))
+    ]
+    for copy in small_copies:
+        copy.start()
 
     def hid_copy(i):
         rows = pl.ds(pl.multiple_of(i * BLK, BLK), BLK)
@@ -135,6 +141,8 @@
             chunk.append(copy)
         pred_copies.append(chunk)
 
+    for copy in small_copies:
+        copy.wait()
     gbuf[:, VS:VP, :] = jnp.zeros((NCH * MEMBERS, VP - VS, 128), BF)
     gout[...] = jnp.zeros_like(gout)
     woT[...] = jnp.zeros_like(woT)
@@ -234,25 +242,6 @@
         copy = remote(csnd.at[b], crcv.at[b], csem, b, sibling)
         copy.start()
         core_copies.append(copy)
-    x1, y1, o1 = [], [], []
-    for b in range(NWB):
-        for cols, value in in_tiles(far_at, core, b):
-            acc[core, b, :, cols] = value + acc[core, b, :, cols]
-        core_copies[b].wait_recv()
-        for q in range(4):
-            rows = slice(q * 128, q * 128 + 128)
-            total = acc[core, b, rows, :] + crcv[b, rows, :].astype(F32)
-            acc[core, b, rows, :] = total
-            s1[b, q] = total.astype(BF)
-        for j in (1, 2, 3):
-            xx, yy = (x + j) % 4, (y + j) % 4
-            copy = remote(s1.at[b, xx, pl.ds(0, 64)], r1a.at[b, x], x1sem.at[b], j, dev(xx, y, z, core))
-            copy.start()
-            x1.append(copy)
-            cols = pl.ds(pl.multiple_of(yy * 128, 128), 128)
-            copy = remote(s1.at[b, :, pl.ds(64, 64), cols], r1b.at[b, y], y1sem.at[b], j, dev(x, yy, z, core))
-            copy.start()
-            y1.append(copy)
     out_term = oacc[...] + out_rows(far_at, far * GB)
     for h8 in range(width // 128):
         turned = jnp.transpose(out_term[:, h8 * 128:h8 * 128 + 128])
@@ -265,40 +254,57 @@
     copy.start()
     core_copies.append(copy)
 
+    for b in range(NWB):
+        for cols, value in in_tiles(far_at, core, b):
+            acc[core, b, :, cols] = value + acc[core, b, :, cols]
+        core_copies[b].wait_recv()
+        for q in range(4):
+            rows = slice(q * 128, q * 128 + 128)
+            total = acc[core, b, rows, :] + crcv[b, rows, :].astype(F32)
+            acc[core, b, rows, :] = total
+            s1a[q, :, b * WB:(b + 1) * WB] = total[0:64, :].astype(BF)
+            for yy in range(4):
+                s1b[yy, q, :, b * 128:b * 128 + 128] = total[64:128, yy * 128:yy * 128 + 128].astype(BF)
     core_copies[NWB].wait_recv()
     for q in range(4):
         rows = slice(q * 128, q * 128 + 128)
         total = oown[core, rows, :] + corcv[rows, :].astype(F32)
         oown[core, rows, :] = total
-        s1o[q] = total.astype(BF)
-    for j in (1, 2, 3):
-        xx = (x + j) % 4
-        copy = remote(s1o.at[xx], r1o.at[x], o1sem, j, dev(xx, y, z, core))
-        copy.start()
-        o1.append(copy)
+        s1a[q, :, width:width + 128] = total[0:64, :].astype(BF)
+        s1a[q, :, width + 128:width + 256] = total[64:128, :].astype(BF)
+    first = []
+    for j in (2, 1, 3):
+        xx, yy = (x + j) % 4, (y + j) % 4
+        copy = remote(s1a.at[xx], r1a.at[x], x1sem, j, dev(xx, y, z, core))
+        copy.start()
+        first.append(copy)
+        copy = remote(s1b.at[yy], r1b.at[y], y1sem, j, dev(x, yy, z, core))
+        copy.start()
+        first.append(copy)
 
     per = points // HB // 2
     lax.fori_loop(0, per, hidden_step, 0)
 
     own_cols = pl.ds(pl.multiple_of(y * 128, 128), 128)
     own_x = pl.multiple_of(x * 128, 128)
-    for copy in x1 + y1 + o1:
+    for copy in first:
         copy.wait_recv()
     for b in range(NWB):
         ta = acc[core, b, pl.ds(own_x, 64), :]
         for j in (1, 2, 3):
-            ta = ta + r1a[b, (x + j) % 4].astype(F32)
+            ta = ta + r1a[(x + j) % 4, :, b * WB:(b + 1) * WB].astype(F32)
         a2[b] = ta
         for q in range(4):
             tb = acc[core, b, q * 128 + 64:q * 128 + 128, own_cols]
             for j in (1, 2, 3):
-                tb = tb + r1b[b, (y + j) % 4, q].astype(F32)
+                tb = tb + r1b[(y + j) % 4, q, :, b * 128:b * 128 + 128].astype(F32)
             b2[b, q] = tb
             s2a[q, 64 * b:64 * b + 64, :] = ta[:, q * 128:q * 128 + 128].astype(BF)
             s2b[q, 64 * b:64 * b + 64, :] = tb.astype(BF)
     to = oown[core, pl.ds(own_x, 128), :]
     for j in (1, 2, 3):
-        to = to + r1o[(x + j) % 4].astype(F32)
+        got = r1a[(x + j) % 4, :, width:width + 256].astype(F32)
+        to = to + jnp.concatenate([got[:, 0:128], got[:, 128:256]], axis=0)
     for q in range(4):
         part = jnp.concatenate([to[zl * 32 + q * 8:zl * 32 + q * 8 + 8, :] for zl in range(4)], axis=0)
         oown[core, q * 32:q * 32 + 32, :] = part
@@ -355,7 +361,7 @@
     for chunk in pred_copies + grad_copies:
         for copy in chunk:
             copy.wait_send()
-    for copy in core_copies + x1 + y1 + o1 + second + third:
+    for copy in core_copies + first + second + third:
         copy.wait_send()
     for copy in fourth:
         copy.wait_recv()
@@ -405,22 +411,23 @@
     results = pl.pallas_call(
         functools.partial(kernel, scale),
         out_shape=tuple(pltpu.VMEM(t.shape, t.dtype) for t in out_types),
-        in_specs=[any_spec, any_spec, any_spec, vmem_spec, vmem_spec, any_spec, vmem_spec],
+        in_specs=[any_spec] * 7,
         out_specs=(vmem_spec, vmem_spec, vmem_spec),
         scratch_shapes=[
+            vm(1, points, dtype=F32), vm(1, V, dtype=F32), vm(V, width),
             vm(points, width), vm(width, width), vm(2, half, points), vm(points, width),
             vm(points, width, dtype=F32), vm(points, width), vm(VP, width),
             vm(NCH, MEMBERS, V, 128), vm(NCH, MEMBERS, V, 128), vm(NCH, V, 128), vm(NCH, MEMBERS, VS, 128),
             vm(NCH * MEMBERS, VP, 128),
             vm(2, NWB, half, WB, dtype=F32), vm(NWB, half, WB), vm(NWB, half, WB),
             vm(VP, width, dtype=F32), vm(half, VP), vm(half, VP), vm(2, half, VP, dtype=F32),
-            vm(NWB, 4, 128, WB), vm(4, 128, VP), vm(NWB, 4, 64, WB), vm(NWB, 4, 4, 64, 128), vm(4, 128, VP),
+            vm(4, 64, width + 256), vm(4, 4, 64, 256), vm(4, 64, width + 256), vm(4, 4, 64, 256),
             vm(NWB, 64, WB, dtype=F32), vm(NWB, 4, 64, 128, dtype=F32),
             vm(4, 160, 128), vm(4, 128, 128), vm(4, 160, 128), vm(4, 128, 128),
             vm(4, 80, 128, dtype=F32), vm(4, 80, 128), vm(8, 80, 128), vm(80, 128), vm(4, 80, 128),
-            sems(3 + MEMBERS, NCH), sems(points // BLK),
+            sems(3 + MEMBERS, 4), sems(points // BLK),
             sems(NCH, 2, MEMBERS), sems(NCH, 2, MEMBERS), sems(2, NWB + 1),
-            sems(NWB, 2, 4), sems(NWB, 2, 4), sems(2, 4), sems(2, 4), sems(2, 4), sems(2, 8), sems(2, 4),
+            sems(2, 4), sems(2, 4), sems(2, 4), sems(2, 4), sems(2, 8), sems(2, 4),
         ],
         compiler_params=pltpu.CompilerParams(
             collective_id=0, has_side_effects=True, vmem_limit_bytes=50 * 1024 * 1024

time: 67.1 us -> 67.5 us (level)
  no operation moved by 1% of the time
where the time goes in v5:
time: 67.5 us; the launch traced here: 67.4 us
  Pallas kernels  66.6 us (99%)
  between operations  0.8 us (1%)
    pallas_call x1, Pallas kernels, shards(): pl.pallas_call(functools.partial(kernel, scale), out_shape=tuple((pltpu.V...  64.5 us
    pallas_call x1, Pallas kernels, shards(): pl.pallas_call(place, out_shape=out_types, in_specs=[vmem_spec] * 3, out_...  2.13 us

profile of v5, /device:TPU:32, one launch (start us, length us, event | category | flops | bytes accessed | tf_op | source)
XLA Modules:
  0.0 67.4 jit_solution(7669146403688679223)
XLA Ops:
  0.6 64.5 %shard_map.94 = (bf16[1,2048,1024]{2,1,0:T(8,128)(2,1)S(1)}, f32[32,1024]{1,0:T(8,128)S(1)}, f32[32,100]{1,0:T(8,128)S(1)}) custom-call(bf16[1,2048,1024]{2,1,0:T(8,128)(2,1)} %hid_hbm.1, bf16[1,100,2048]{2,1,0:T(8,128)(2,1)} %pred_hbm.1, bf16[100,2048]{1,0:T(8,128)(2,1)} %tgt_hbm.1, f32[1,2048]{1,0:T(1,128)} %bitcast.4, f32[1,100]{1,0:T(1,128)} %bitcast.5, ...), custom_call_target="tpu_custom_call" | custom-call | tf_op jit(solution)/shard_map/pallas_call | solution.py:411
  65.1 2.1 %shard_map.95 = (bf16[1,2048,1024]{2,1,0:T(8,128)(2,1)}, f32[32,1024]{1,0:T(8,128)}, f32[32,100]{1,0:T(8,128)}) custom-call(bf16[1,2048,1024]{2,1,0:T(8,128)(2,1)S(1)} %get-tuple-element.6.hg_in, f32[32,1024]{1,0:T(8,128)S(1)} %get-tuple-element.7.in_in, f32[32,100]{1,0:T(8,128)S(1)} %get-tuple-element.8.out_in), custom_call_target="tpu_custom_call" | custom-call | tf_op jit(solution)/shard_map/pallas_call | solution.py:436

commit v6 on v5

--- a/solution.py
+++ b/solution.py
@@ -14,7 +14,7 @@
 V = 100
 VS = 112
 VP = 128
-NCH = 2
+NCH = 1
 BLK = 512
 HB = 1024
 GB = 4
@@ -45,6 +45,7 @@
     points = hid.shape[0]
     width = hid.shape[1]
     half = points // NCH
+    pb = half // MEMBERS
     m = lax.axis_index("member")
     g = lax.axis_index("grid")
     y, z_hi = m // 2, m % 2
@@ -94,11 +95,11 @@
 
     own_copies, source_copies = [], []
     for c in range(NCH):
-        mine = pl.ds(pl.multiple_of(c * half + 128 * mine_p, 128), 128)
+        mine = pl.ds(pl.multiple_of(c * half + pb * mine_p, pb), pb)
         own_copies.append(pltpu.make_async_copy(pred_hbm.at[0, :, mine], prcv.at[c, mine_p], lsem.at[1, c]))
         own_copies.append(pltpu.make_async_copy(tgt_hbm.at[:, mine], tgt.at[c], lsem.at[2, c]))
         for k in range(MEMBERS):
-            cols = pl.ds(c * half + 128 * k, 128)
+            cols = pl.ds(c * half + pb * k, pb)
             source_copies.append(pltpu.make_async_copy(pred_hbm.at[0, :, cols], psrc.at[c, k], lsem.at[3 + k, c]))
     for copy in source_copies + own_copies:
         copy.start()
@@ -143,7 +144,7 @@
 
     for copy in small_copies:
         copy.wait()
-    gbuf[:, VS:VP, :] = jnp.zeros((NCH * MEMBERS, VP - VS, 128), BF)
+    gbuf[:, VS:VP, :] = jnp.zeros((NCH * MEMBERS, VP - VS, pb), BF)
     gout[...] = jnp.zeros_like(gout)
     woT[...] = jnp.zeros_like(woT)
     woT[0:V, :] = wout_t[...]
@@ -159,7 +160,7 @@
         own_copies[2 * c + 1].wait()
         for copy in pred_copies[c]:
             copy.wait_recv()
-        cols = pl.ds(pl.multiple_of(c * half + 128 * mine_p, 128), 128)
+        cols = pl.ds(pl.multiple_of(c * half + pb * mine_p, pb), pb)
         weight = vcol * area[:, cols]
         rounded = weight.astype(BF).astype(F32)
         aim = tgt[c].astype(F32)
@@ -183,7 +184,7 @@
         grad_copies.append(chunk)
 
     def back(i, carry):
-        rows = pl.ds(pl.multiple_of(i * (GB * 128), GB * 128), GB * 128)
+        rows = pl.ds(pl.multiple_of(i * (GB * pb), GB * pb), GB * pb)
         turned = jnp.concatenate([jnp.transpose(gbuf[i * GB + k]) for k in range(GB)], axis=0)
         for n in range(0, width, 512):
             pg[rows, n:n + 512] = (dot(turned, woT[:, n:n + 512]) * gp[rows, n:n + 512]).astype(BF)
@@ -199,7 +200,7 @@
     sibling = dev(x, y, z, other)
     last = NCH - 1
 
-    group = GB * 128
+    group = GB * pb
 
     def in_tiles(at, which, b):
         rows = pl.ds(*at)
@@ -207,7 +208,7 @@
             yield slice(n, n + 256), dot(hT[which, :, rows], pg[rows, b * WB + n:b * WB + n + 256])
 
     def out_rows(at, first):
-        blocks = [gbuf[first + k] for k in range(at[1] // 128)]
+        blocks = [gbuf[first + k] for k in range(at[1] // pb)]
         return dot(jnp.concatenate(blocks, axis=1), act[pl.ds(*at), :])
 
     def add_terms(at, first, start):
@@ -228,7 +229,7 @@
         copy.wait_recv()
     near = last * 2 + z_hi
     back(near, 0)
-    add_terms((pl.multiple_of(near * group, group), group), near * GB, False)
+    add_terms((pl.multiple_of(near * group, group), group), near * GB, last == 0)
     for copy in grad_copies[last][:fars]:
         copy.wait_recv()
     far = last * 2 + 1 - z_hi
@@ -408,6 +409,7 @@
         jax.ShapeDtypeStruct((share, V), F32),
     )
     half = width // 2
+    pb = points // (NCH * MEMBERS)
     results = pl.pallas_call(
         functools.partial(kernel, scale),
         out_shape=tuple(pltpu.VMEM(t.shape, t.dtype) for t in out_types),
@@ -417,8 +419,8 @@
             vm(1, points, dtype=F32), vm(1, V, dtype=F32), vm(V, width),
             vm(points, width), vm(width, width), vm(2, half, points), vm(points, width),
             vm(points, width, dtype=F32), vm(points, width), vm(VP, width),
-            vm(NCH, MEMBERS, V, 128), vm(NCH, MEMBERS, V, 128), vm(NCH, V, 128), vm(NCH, MEMBERS, VS, 128),
-            vm(NCH * MEMBERS, VP, 128),
+            vm(NCH, MEMBERS, V, pb), vm(NCH, MEMBERS, V, pb), vm(NCH, V, pb), vm(NCH, MEMBERS, VS, pb),
+            vm(NCH * MEMBERS, VP, pb),
             vm(2, NWB, half, WB, dtype=F32), vm(NWB, half, WB), vm(NWB, half, WB),
             vm(VP, width, dtype=F32), vm(half, VP), vm(half, VP), vm(2, half, VP, dtype=F32),
             vm(4, 64, width + 256), vm(4, 4, 64, 256), vm(4, 64, width + 256), vm(4, 4, 64, 256),

time: 67.5 us -> 65.5 us (0.970)
  Pallas kernels: 66.6 us -> 64.6 us
    pallas_call x1, Pallas kernels: 64.5 us -> 62.5 us  [shards(): pl.pallas_call(functools.partial(kernel, scale), out_shape=tuple((pltpu.V...]
where the time goes in v6:
time: 65.5 us; the launch traced here: 65.4 us
  Pallas kernels  64.6 us (99%)
  between operations  0.8 us (1%)
    pallas_call x1, Pallas kernels, shards(): pl.pallas_call(functools.partial(kernel, scale), out_shape=tuple((pltpu.V...  62.5 us
    pallas_call x1, Pallas kernels, shards(): pl.pallas_call(place, out_shape=out_types, in_specs=[vmem_spec] * 3, out_...  2.13 us

profile of v6, /device:TPU:32, one launch (start us, length us, event | category | flops | bytes accessed | tf_op | source)
XLA Modules:
  0.0 65.4 jit_solution(9374114053804567345)
XLA Ops:
  0.6 62.5 %shard_map.94 = (bf16[1,2048,1024]{2,1,0:T(8,128)(2,1)S(1)}, f32[32,1024]{1,0:T(8,128)S(1)}, f32[32,100]{1,0:T(8,128)S(1)}) custom-call(bf16[1,2048,1024]{2,1,0:T(8,128)(2,1)} %hid_hbm.1, bf16[1,100,2048]{2,1,0:T(8,128)(2,1)} %pred_hbm.1, bf16[100,2048]{1,0:T(8,128)(2,1)} %tgt_hbm.1, f32[1,2048]{1,0:T(1,128)} %bitcast.4, f32[1,100]{1,0:T(1,128)} %bitcast.5, ...), custom_call_target="tpu_custom_call" | custom-call | tf_op jit(solution)/shard_map/pallas_call | solution.py:413
  63.1 2.1 %shard_map.95 = (bf16[1,2048,1024]{2,1,0:T(8,128)(2,1)}, f32[32,1024]{1,0:T(8,128)}, f32[32,100]{1,0:T(8,128)}) custom-call(bf16[1,2048,1024]{2,1,0:T(8,128)(2,1)S(1)} %get-tuple-element.6.hg_in, f32[32,1024]{1,0:T(8,128)S(1)} %get-tuple-element.7.in_in, f32[32,100]{1,0:T(8,128)S(1)} %get-tuple-element.8.out_in), custom_call_target="tpu_custom_call" | custom-call | tf_op jit(solution)/shard_map/pallas_call | solution.py:438

commit v7 on v6

--- a/solution.py
+++ b/solution.py
@@ -176,7 +176,7 @@
             grad = weight * s / MEMBERS - (rounded * counts[k]) / (MEMBERS * (MEMBERS - 1))
             gout[c, k, :V, :] = grad.astype(BF)
         chunk = []
-        for j, p, to in members_far_first:
+        for j, p, to in members_far_first[fars:] + members_far_first[:fars]:
             copy = remote(gout.at[c, p], gbuf.at[c * MEMBERS + mine_p, pl.ds(0, VS)], gsem.at[c], j, member_dev(to))
             copy.start()
             chunk.append(copy)
@@ -225,12 +225,12 @@
             back(c * (MEMBERS // GB) + i, 0)
         add_terms((c * half, half), c * MEMBERS, c == 0)
 
-    for copy in grad_copies[last][fars:]:
+    for copy in grad_copies[last][:MEMBERS - 1 - fars]:
         copy.wait_recv()
     near = last * 2 + z_hi
     back(near, 0)
     add_terms((pl.multiple_of(near * group, group), group), near * GB, last == 0)
-    for copy in grad_copies[last][:fars]:
+    for copy in grad_copies[last][MEMBERS - 1 - fars:]:
         copy.wait_recv()
     far = last * 2 + 1 - z_hi
     far_at = (pl.multiple_of(far * group, group), group)

time: 65.5 us -> 65.6 us (level)
  no operation moved by 1% of the time
where the time goes in v7:
time: 65.6 us; the launch traced here: 65.4 us
  Pallas kernels  64.6 us (98%)
  between operations  0.8 us (1%)
    pallas_call x1, Pallas kernels, shards(): pl.pallas_call(functools.partial(kernel, scale), out_shape=tuple((pltpu.V...  62.5 us
    pallas_call x1, Pallas kernels, shards(): pl.pallas_call(place, out_shape=out_types, in_specs=[vmem_spec] * 3, out_...  2.13 us

profile of v7, /device:TPU:32, one launch (start us, length us, event | category | flops | bytes accessed | tf_op | source)
XLA Modules:
  0.0 65.4 jit_solution(18231821411267070748)
XLA Ops:
  0.6 62.5 %shard_map.94 = (bf16[1,2048,1024]{2,1,0:T(8,128)(2,1)S(1)}, f32[32,1024]{1,0:T(8,128)S(1)}, f32[32,100]{1,0:T(8,128)S(1)}) custom-call(bf16[1,2048,1024]{2,1,0:T(8,128)(2,1)} %hid_hbm.1, bf16[1,100,2048]{2,1,0:T(8,128)(2,1)} %pred_hbm.1, bf16[100,2048]{1,0:T(8,128)(2,1)} %tgt_hbm.1, f32[1,2048]{1,0:T(1,128)} %bitcast.4, f32[1,100]{1,0:T(1,128)} %bitcast.5, ...), custom_call_target="tpu_custom_call" | custom-call | tf_op jit(solution)/shard_map/pallas_call | solution.py:413
  63.1 2.1 %shard_map.95 = (bf16[1,2048,1024]{2,1,0:T(8,128)(2,1)}, f32[32,1024]{1,0:T(8,128)}, f32[32,100]{1,0:T(8,128)}) custom-call(bf16[1,2048,1024]{2,1,0:T(8,128)(2,1)S(1)} %get-tuple-element.6.hg_in, f32[32,1024]{1,0:T(8,128)S(1)} %get-tuple-element.7.in_in, f32[32,100]{1,0:T(8,128)S(1)} %get-tuple-element.8.out_in), custom_call_target="tpu_custom_call" | custom-call | tf_op jit(solution)/shard_map/pallas_call | solution.py:438
